TPU v7x, 128 devices: a whole 4x4x4 slice. The times are simulated.
128 devices in a mesh: cand: 4 (over y_lo, core), ctx: 32 (over z, y_hi, x).
Axes of the slice: x: 4, y: 4 (y_hi: 2, y_lo: 2; y = y_hi * 2 + y_lo), z: 4, core: 2. Of those that a mesh axis runs over, the one named last changes fastest.
Arguments:
- history: bfloat16 [8, 65536, 256], P(None, 'ctx'), may hold values from -6 to 6
- candidates: bfloat16 [8, 2048, 256], P(None, 'cand'), may hold values from -70 to 70
- short_hist: bfloat16 [8, 256, 256], replicated, may hold values from -6 to 6
- lengths: int32 [8], replicated, may hold values from 8192 to 65536, as said below
- pad_mask: int32 [8, 65536], P(None, 'ctx'), may hold values 0 or 1
- short_mask: int32 [8, 256], replicated, may hold values 0 or 1
- query_gain: float32 [256], replicated, may hold values from 0.5 to 2
- value_weight: bfloat16 [256, 256], replicated, may hold values from -0.375 to 0.375
- head_weight: bfloat16 [256, 256], replicated, may hold values from -0.375 to 0.375
- head_vector: float32 [256], replicated, may hold values from -1.5 to 1.5
- pair_weight: float32 [256, 128], replicated, may hold values from -0.375 to 0.375
- event_weight: float32 [256, 128], replicated, may hold values from -0.375 to 0.375
- scoring_bias: float32 [128], replicated, may hold values from -3 to 3
- weigher: float32 [128], replicated, may hold values from -0.5 to 0.5
- pooling_weight: float32 [256, 256], replicated, may hold values from -0.046875 to 0.046875
- itemwise_weight: float32 [256, 256], replicated, may hold values from -0.375 to 0.375
- hidden_bias: float32 [256], replicated, may hold values from -3 to 3
- output_vector: float32 [256], replicated, may hold values from -1.5 to 1.5
Outputs:
- teacher_logits: float32 [8, 2048], P(None, ('cand', 'ctx'))
- pair_grad: float32 [256, 128], replicated
- event_grad: float32 [256, 128], replicated
- scoring_grad: float32 [128], replicated
- weigher_grad: float32 [128], replicated
- pooling_grad: float32 [256, 256], replicated
- itemwise_grad: float32 [256, 256], replicated
- hidden_grad: float32 [256], replicated
- output_grad: float32 [256], replicated
Inputs may be any that keep to these rules, and one draw needn't show every extreme that they name: `lengths`: valid history events of each user, counted from the first position.
All inputs are finite; a program needn't handle non-finite values. No bound on the sum of `pad_mask` on one device may be relied on, other than what follows from the above.
Results may differ from a plain program's by a relative error of at most 0.029.
Values sent between devices are 32-bit elements; how exact they have to be, the bound alone decides.
A program may use at most 384 MiB of HBM per device.

v0:
```python
import math

import jax
import jax.numpy as jnp
from jax import lax
from jax.sharding import PartitionSpec as P

NEG_FILL = -1e30
SOFT_CAP = 10.0
HIGHEST = lax.Precision.HIGHEST


def capped(logits):
    return SOFT_CAP * jnp.tanh(logits / SOFT_CAP)


def teacher_head(pooled, cand_rows, head_weight, head_vector):
    normed = pooled * lax.rsqrt(jnp.mean(pooled * pooled, axis=-1, keepdims=True) + 1e-06)
    mixed = (normed * cand_rows.astype(jnp.float32)).astype(jnp.bfloat16)
    hidden = jax.nn.gelu(
        jnp.einsum("ure,eh->urh", mixed, head_weight, preferred_element_type=jnp.float32)
    )
    return capped(jnp.sum(hidden * head_vector, axis=-1))


def student(params, short_f, short_ok, cand_f):
    (
        pair_weight,
        event_weight,
        scoring_bias,
        weigher,
        pooling_weight,
        itemwise_weight,
        hidden_bias,
        output_vector,
    ) = params
    event_part = jnp.einsum("use,ea->usa", short_f, event_weight, precision=HIGHEST)
    pairs = cand_f[:, :, None, :] * short_f[:, None, :, :]
    activation = jax.nn.relu(
        jnp.einsum("urse,ea->ursa", pairs, pair_weight, precision=HIGHEST)
        + event_part[:, None]
        + scoring_bias
    )
    attention = jnp.einsum("ursa,a->urs", activation, weigher, precision=HIGHEST)
    attention = jnp.where(short_ok[:, None, :], attention, 0.0)
    interest = jnp.einsum("urs,use->ure", attention, short_f, precision=HIGHEST)
    hidden = jax.nn.gelu(
        jnp.einsum("ure,eh->urh", interest, pooling_weight, precision=HIGHEST)
        + jnp.einsum("ure,eh->urh", cand_f, itemwise_weight, precision=HIGHEST)
        + hidden_bias
    )
    return capped(jnp.einsum("urh,h->ur", hidden, output_vector, precision=HIGHEST))


def body(
    history,
    candidates,
    short_hist,
    lengths,
    pad_mask,
    short_mask,
    query_gain,
    value_weight,
    head_weight,
    head_vector,
    pair_weight,
    event_weight,
    scoring_bias,
    weigher,
    pooling_weight,
    itemwise_weight,
    hidden_bias,
    output_vector,
):
    members = history.shape[0]
    hist_dev = history.shape[1]
    width = history.shape[2]
    cand_dev = candidates.shape[1]
    ctx_count = lax.axis_size("ctx")
    ctx_place = lax.axis_index("ctx")
    own_rows = cand_dev // ctx_count
    own_start = ctx_place * own_rows
    positions = ctx_place * hist_dev + jnp.arange(hist_dev, dtype=jnp.int32)
    event_ok = (positions[None, :] < lengths[:, None]) & (
        (pad_mask == 1) | (positions[None, :] == 0)
    )
    query = (candidates.astype(jnp.float32) * query_gain).astype(jnp.bfloat16)
    values = jnp.einsum(
        "uhe,ef->uhf", history, value_weight, preferred_element_type=jnp.float32
    ).astype(jnp.bfloat16)
    scores = jnp.einsum("uce,uhe->uch", query, history, preferred_element_type=jnp.float32) * (
        1.0 / math.sqrt(width)
    )
    ok_wide = event_ok[:, None, :]
    block_max = jnp.max(jnp.where(ok_wide, scores, NEG_FILL), axis=2)
    block_exp = jnp.where(ok_wide, jnp.exp(scores - block_max[:, :, None]), 0.0)
    block_total = jnp.sum(block_exp, axis=2)
    block_value = jnp.einsum(
        "uch,uhf->ucf", block_exp.astype(jnp.bfloat16), values, preferred_element_type=jnp.float32
    )
    own_cands = lax.dynamic_slice_in_dim(candidates, own_start, own_rows, 1)
    highest = lax.pmax(block_max, "ctx")
    factor = jnp.exp(block_max - highest)
    summed = lax.psum((block_total * factor, block_value * factor[:, :, None]), "ctx")
    totals = lax.dynamic_slice_in_dim(summed[0], own_start, own_rows, 1)
    weighted = lax.dynamic_slice_in_dim(summed[1], own_start, own_rows, 1)
    pooled = weighted / totals[:, :, None]
    teacher_logits = teacher_head(pooled, own_cands, head_weight, head_vector)
    short_len = short_hist.shape[1]
    short_pos = jnp.arange(short_len, dtype=jnp.int32)
    short_ok = (short_mask == 1) | (short_pos[None, :] == 0)
    short_f = short_hist.astype(jnp.float32)
    cand_f = own_cands.astype(jnp.float32)
    params = (
        pair_weight,
        event_weight,
        scoring_bias,
        weigher,
        pooling_weight,
        itemwise_weight,
        hidden_bias,
        output_vector,
    )
    loss_scale = math.sqrt(cand_dev * lax.axis_size("cand") / members)
    teacher_exp = jnp.exp(teacher_logits)
    student_logits, pull = jax.vjp(
        lambda param_set: student(param_set, short_f, short_ok, cand_f), params
    )
    student_exp = jnp.exp(student_logits)
    list_sums = lax.psum(
        (jnp.sum(student_exp, axis=1), jnp.sum(teacher_exp, axis=1)), ("cand", "ctx")
    )
    logit_grad = loss_scale * (
        student_exp / list_sums[0][:, None] - teacher_exp / list_sums[1][:, None]
    )
    local = pull(logit_grad)[0]
    grads = lax.psum(
        (local[0], local[1], local[2], local[3], local[4], local[5], local[6], local[7]),
        ("cand", "ctx"),
    )
    return (
        teacher_logits,
        grads[0],
        grads[1],
        grads[2],
        grads[3],
        grads[4],
        grads[5],
        grads[6],
        grads[7],
    )


def solution(mesh):
    placed = (
        P(None, "ctx", None),
        P(None, "cand", None),
        P(),
        P(),
        P(None, "ctx"),
        P(),
        P(),
        P(),
        P(),
        P(),
        P(),
        P(),
        P(),
        P(),
        P(),
        P(),
        P(),
        P(),
    )
    return jax.shard_map(
        body,
        mesh=mesh,
        in_specs=placed,
        out_specs=(P(None, ("cand", "ctx")), P(), P(), P(), P(), P(), P(), P(), P()),
        check_vma=False,
    )
```

profile of v0, /device:TPU:1, one launch (start us, length us, event | category | flops | bytes accessed | tf_op | source)
XLA Modules:
  0.0 879.1 jit_solution(16289867981389219487)
XLA Ops:
  7.2 0.0 copy-start
  7.2 0.0 all-reduce.6.cloned.1.call-start
  7.3 0.9 or_and_fusion
  8.2 16.1 %select_reduce_fusion = (f32[8,512]{1,0:T(8,128)S(1)}, f32[8,512,2048]{2,1,0:T(8,128)}) fusion(pred[8,2048]{1,0:T(8,128)(4,1)S(1)} %or_and_fusion, bf16[8,2048,256]{2,1,0:T(8,128)(2,1)} %param.18, bf16[8,512,256]{2,1,0:T(8,128)(2,1)} %param.19, f32[256]{0:T(256)} %param.24), kind=kOutput, calls=%fused_computation.5 | convolution fusion | flops 4323274752 | bytes 44073984 | tf_op jit(solution)/shard_map/uce,uhe->uch/dot_general | solution.py:91
  24.3 157.7 %pmax.7 = f32[8,512]{1,0:T(8,128)S(1)} all-reduce(f32[8,512]{1,0:T(8,128)S(1)} %get-tuple-element.43), channel_id=1, replica_groups=mesh['cand'=4,'ctx'=32] {'ctx'}, use_global_device_ids=true, to_apply=%region_1.2 | all-reduce | flops 4096 | bytes 32768 | tf_op jit(solution)/shard_map/pmax | solution.py:102
  182.0 14.6 %fusion.4 = f32[8,512]{1,0:T(8,128)S(1)} fusion(f32[8,512,2048]{2,1,0:T(8,128)} %get-tuple-element.44, f32[8,512]{1,0:T(8,128)S(1)} %get-tuple-element.43, pred[8,2048]{1,0:T(8,128)(4,1)S(1)} %or_and_fusion), kind=kLoop, calls=%fused_computation.6 | loop fusion | flops 33550336 | bytes 33603584 | tf_op jit(solution)/shard_map/reduce_sum | solution.py:97
  196.7 0.0 copy-done.11
  196.7 0.0 copy-start.2
  196.7 0.0 copy-start.4
  196.7 0.0 copy-start.3
  196.7 0.0 copy-start.6
  196.7 0.0 copy-start.8
  196.7 0.0 copy-start.12
  196.7 17.4 %fusion.35 = f32[8,512,256]{2,1,0:T(8,128)} fusion(bf16[8,2048,256]{2,1,0:T(8,128)(2,1)} %param.18, f32[8,512,2048]{2,1,0:T(8,128)} %get-tuple-element.44, f32[8,512]{1,0:T(8,128)S(1)} %get-tuple-element.43, pred[8,2048]{1,0:T(8,128)(4,1)S(1)} %or_and_fusion, f32[8,512]{1,0:T(8,128)S(1)} %get-tuple-element.42, bf16[256,256]{1,0:T(8,128)(2,1)S(1)} %copy-done.11), kind=kOutput, calls=%fused_computation.40 | convolution fusion | flops 6481248256 | bytes 46317568 | tf_op jit(solution)/shard_map/uch,uhf->ucf/dot_general | solution.py:98
  214.1 0.0 all-reduce.6.cloned.1.call-update
  214.2 0.0 all-reduce.8.cloned.1.call-start
  214.2 151.8 %psum.85 = f32[8,512]{1,0:T(8,128)S(1)} all-reduce(f32[8,512]{1,0:T(8,128)S(1)} %get-tuple-element.41), channel_id=1, replica_groups=mesh['cand'=4,'ctx'=32] {'ctx'}, use_global_device_ids=true, to_apply=%region_4.5 | all-reduce | flops 4096 | bytes 32768 | tf_op jit(solution)/shard_map/psum | solution.py:104
  366.0 0.9 dynamic-slice_convert_fusion
  366.8 0.1 constant_dynamic-slice_fusion
  366.9 0.0 copy-done.2
  366.9 1.6 copy.30
  368.6 1.0 fusion.74
  369.6 0.0 copy-done.3
  369.6 0.0 copy-start.7
  369.6 1.1 fusion.49
  370.7 72.7 %fusion.22 = (u16[8,256,128]{2,1,0:T(8,128)(2,1)S(1)}, f32[8,16,256,128]{3,2,1,0:T(8,128)S(1)}) fusion(f32[128]{0:T(128)S(1)} %copy-done.8, f32[8,256,128]{2,1,0:T(8,128)S(1)} %fusion.74, f32[256,128]{1,0:T(8,128)S(1)} %copy-done.12, f32[8,256,256]{1,2,0:T(8,128)} %copy.30, f32[8,16,256]{2,1,0:T(8,128)S(1)} %dynamic-slice_convert_fusion), kind=kOutput, calls=%fused_computation.27 | convolution fusion | flops 12922388480 | bytes 20709888 | tf_op jit(solution)/shard_map/jvp(urse,ea->ursa)/dot_general | solution.py:40
  443.5 0.0 copy-start.1
  443.5 0.0 copy-start.9
  443.5 0.0 copy-start.10
  443.5 0.0 copy-start.13
  443.5 5.7 copy-done.1
  449.2 15.8 %fusion.20 = f32[1,8,16,256]{3,0,2,1:T(1,128)S(1)} fusion(f32[8,16,256,128]{3,2,1,0:T(8,128)S(1)} %get-tuple-element.46, f32[128]{0:T(128)S(1)} %copy-done.8, f32[8,256,128]{2,1,0:T(8,128)S(1)} %fusion.74, f32[128]{0:T(128)S(1)} %copy-done.7), kind=kOutput, calls=%fused_computation.25 | convolution fusion | flops 62914560 | bytes 17957888 | tf_op jit(solution)/shard_map/jvp(ursa,a->urs)/dot_general | solution.py:44
  465.0 0.5 fusion.73
  465.5 0.0 copy-done
  465.5 0.0 copy-done.9
  465.5 0.3 fusion.42
  465.8 0.0 copy-done.10
  465.8 0.6 fusion.85
  466.4 4.8 and_convert_fusion
  471.2 109.5 %all-reduce.6.cloned.1.call-done = f32[8,512,256]{2,1,0:T(8,128)} async-done(((f32[8,512,256]{2,1,0:T(8,128)}), f32[8,512,256]{2,1,0:T(8,128)}) %all-reduce.6.cloned.1.call-update) | async-done | bytes 4194320 | tf_op jit(solution)/shard_map/psum | solution.py:104
  580.7 1.1 multiply_reduce_fusion
  581.8 1.3 fusion.71
  583.1 0.2 exponential_reduce_fusion
  583.3 0.0 copy-start.5
  583.3 85.9 %all-reduce.1 = (f32[8]{0:T(128)S(1)}, f32[8]{0:T(128)S(1)}) all-reduce(f32[8]{0:T(128)S(1)} %get-tuple-element.39, f32[8]{0:T(128)S(1)} %get-tuple-element.47), channel_id=1, replica_groups=mesh['cand'=4,'ctx'=32] {'cand','ctx'}, use_global_device_ids=true, to_apply=%region_10.11 | all-reduce | flops 16 | bytes 128 | tf_op jit(solution)/shard_map/psum | solution.py:130
  669.2 0.1 multiply_multiply_fusion.8
  669.3 0.4 fusion.51
  669.7 1.9 convolution_bitcast_fusion
  671.7 1.2 convolution_bitcast_fusion.1
  672.8 0.9 convolution_select_fusion
  673.8 5.0 fusion.8
  678.8 1.7 convolution_bitcast_fusion.2
  680.4 7.8 multiply_select_fusion.7
  688.3 32.3 %fusion.43 = f32[256,128]{1,0:T(8,128)} fusion(f32[8,256,256]{1,2,0:T(8,128)} %copy.30, f32[8,16,256]{2,1,0:T(8,128)S(1)} %dynamic-slice_convert_fusion, f32[8,16,256,128]{3,2,1,0:T(8,128)} %multiply_select_fusion.7), kind=kOutput, calls=%fused_computation.47 | convolution fusion | flops 12893290496 | bytes 19136512 | tf_op jit(solution)/shard_map/transpose(jvp(urse,ea->ursa))/dot_general | solution.py:40
  720.6 0.0 all-reduce.8.cloned.1.call-update
  720.7 13.3 %fusion.46 = f32[128]{0:T(128)S(1)} fusion(f32[8,16,256,128]{3,2,1,0:T(8,128)} %copy-done.1, f32[128]{0:T(128)S(1)} %copy-done.8, f32[8,256,128]{2,1,0:T(8,128)S(1)} %fusion.74, f32[8,16,256,1]{2,1,0,3:T(8,128)S(1)} %bitcast.72), kind=kOutput, calls=%fused_computation.50 | convolution fusion | flops 62914560 | bytes 17957888 | tf_op jit(solution)/shard_map/transpose(jvp(ursa,a->urs))/dot_general | solution.py:44
  734.0 0.1 fusion.107
  734.1 0.2 fusion.84
  734.3 63.9 %all-reduce = (f32[128]{0:T(128)}, f32[128]{0:T(128)}, f32[256]{0:T(256)}, f32[256]{0:T(256)}) all-reduce(f32[128]{0:T(128)S(1)} %get-tuple-element.27, f32[128]{0:T(128)S(1)} %fusion.46, f32[256]{0:T(256)S(1)} %fusion.107, f32[256]{0:T(256)S(1)} %bitcast.77), channel_id=1, replica_groups=mesh['cand'=4,'ctx'=32] {'cand','ctx'}, use_global_device_ids=true, to_apply=%region_15.16 | all-reduce | flops 768 | bytes 6144 | tf_op jit(solution)/shard_map/psum | solution.py:137
  798.2 67.1 %all-reduce.8.cloned.1.call-done = (f32[256,128]{1,0:T(8,128)}, f32[256,128]{0,1:T(8,128)}, f32[256,256]{1,0:T(8,128)}, f32[256,256]{1,0:T(8,128)}) async-done(((f32[256,128]{1,0:T(8,128)}, f32[256,128]{0,1:T(8,128)}, f32[256,256]{1,0:T(8,128)}, f32[256,256]{1,0:T(8,128)}), (f32[256,128]{1,0:T(8,128)}, f32[256,128]{0,1:T(8,128)}, f32[256,256]{1,0:T(8,128)}, ...) | async-done | bytes 786448 | tf_op jit(solution)/shard_map/psum | solution.py:137
  865.4 1.7 copy.33
  867.0 1.6 copy.55
  868.6 1.7 copy.56
  870.2 1.7 copy.57
  (14 shorter events, 0.1 us)
Async XLA Ops:
  7.2 458.3 %copy-start = (f32[256,256]{1,0:T(8,128)S(1)}, f32[256,256]{1,0:T(8,128)}, u32[]{:S(2)}) copy-start(f32[256,256]{1,0:T(8,128)} %param.32) | copy-start | bytes 786436
  7.2 573.5 %all-reduce.6.cloned.1.call-start = ((), (), s32[]{:S(2)}) async-start(), calls=%async_computation | async-start | bytes 8388608 | tf_op jit(solution)/shard_map/psum | solution.py:104
  182.0 14.6 %copy-start.11 = (bf16[256,256]{1,0:T(8,128)(2,1)S(1)}, bf16[256,256]{1,0:T(8,128)(2,1)}, u32[]{:S(2)}) copy-start(bf16[256,256]{1,0:T(8,128)(2,1)} %param.25) | copy-start | bytes 393220
  196.7 170.3 %copy-start.2 = (bf16[8,256,256]{2,1,0:T(8,128)(2,1)S(1)}, bf16[8,256,256]{2,1,0:T(8,128)(2,1)}, u32[]{:S(2)}) copy-start(bf16[8,256,256]{2,1,0:T(8,128)(2,1)} %param.20) | copy-start | bytes 3145732
  196.7 171.9 %copy-start.4 = (f32[256,128]{1,0:T(8,128)S(1)}, f32[256,128]{1,0:T(8,128)}, u32[]{:S(2)}) copy-start(f32[256,128]{1,0:T(8,128)} %param.29) | copy-start | bytes 393220
  196.7 172.9 %copy-start.3 = (f32[256,256]{1,0:T(8,128)S(1)}, f32[256,256]{1,0:T(8,128)}, u32[]{:S(2)}) copy-start(f32[256,256]{1,0:T(8,128)} %param.33) | copy-start | bytes 786436
  196.7 174.0 %copy-start.6 = (s32[8,256]{1,0:T(8,128)S(1)}, s32[8,256]{1,0:T(8,128)}, u32[]{:S(2)}) copy-start(s32[8,256]{1,0:T(8,128)} %param.23) | copy-start | bytes 24580
  196.7 174.0 %copy-start.8 = (f32[128]{0:T(128)S(1)}, f32[128]{0:T(128)}, u32[]{:S(2)}) copy-start(f32[128]{0:T(128)} %param.30) | copy-start | bytes 1540
  196.7 174.0 %copy-start.12 = (f32[256,128]{1,0:T(8,128)S(1)}, f32[256,128]{1,0:T(8,128)}, u32[]{:S(2)}) copy-start(f32[256,128]{1,0:T(8,128)} %param.28) | copy-start | bytes 393220
  214.2 651.2 %all-reduce.8.cloned.1.call-start = ((), (), s32[]{:S(2)}) async-start(), calls=%async_computation.1 | async-start | bytes 1572864 | tf_op jit(solution)/shard_map/psum | solution.py:137
  369.6 79.6 %copy-start.7 = (f32[128]{0:T(128)S(1)}, f32[128]{0:T(128)}, u32[]{:S(2)}) copy-start(f32[128]{0:T(128)} %param.31) | copy-start | bytes 1540
  443.5 5.7 copy-start.1
  443.5 22.0 %copy-start.9 = (f32[256]{0:T(256)S(1)}, f32[256]{0:T(256)}, u32[]{:S(2)}) copy-start(f32[256]{0:T(256)} %param.34) | copy-start | bytes 3076
  443.5 22.3 %copy-start.10 = (f32[256]{0:T(256)S(1)}, f32[256]{0:T(256)}, u32[]{:S(2)}) copy-start(f32[256]{0:T(256)} %param.35) | copy-start | bytes 3076
  443.5 138.3 %copy-start.13 = (f32[256]{0:T(256)S(1)}, f32[256]{0:T(256)}, u32[]{:S(2)}) copy-start(f32[256]{0:T(256)} %param.27) | copy-start | bytes 3076
  583.3 137.3 %copy-start.5 = (f32[8,16]{1,0:T(8,128)}, f32[8,16]{1,0:T(8,128)S(1)}, u32[]{:S(2)}) copy-start(f32[8,16]{1,0:T(8,128)S(1)} %get-tuple-element.48) | copy-start | bytes 1540
Sparse Core Ops, SparseCore 0:
  214.3 366.3 all-reduce.5
  720.8 144.5 all-reduce.7
where the time goes:
time: 886 us; the launch traced here: 879 us
  blocking collectives  459 us (52%)
  matrix products  179 us (20%)
  waiting for transfers between devices  177 us (20%)
  other arithmetic  35.5 us (4%)
  between operations  14.7 us (2%)
  local copies, waits for them, and re-layouts  14 us (2%)
    pmax x1, blocking collectives, body(): highest = lax.pmax(block_max, 'ctx')  158 us
    psum x1, blocking collectives, body(): lax.psum((block_total * factor, block_value * factor[:, :, None]), 'ctx')  152 us
    psum x1, waiting for transfers between devices, body(): lax.psum((block_total * factor, block_value * factor[:, :, None]), 'ctx')  110 us
    dot_general x2, matrix products, student(): jnp.einsum('urse,ea->ursa', pairs, pair_weight, precision=HIGHEST)  105 us
    psum x1, blocking collectives, body(): lax.psum((jnp.sum(student_exp, axis=1), jnp.sum(teacher_exp, axis=1)), ('...  85.9 us
    psum x1, waiting for transfers between devices, body(): lax.psum((local[0], local[1], local[2], local[3], local[4], local[5], loc...  67.1 us
    psum x1, blocking collectives, body(): lax.psum((local[0], local[1], local[2], local[3], local[4], local[5], loc...  63.9 us
    dot_general x2, matrix products, student(): jnp.einsum('ursa,a->urs', activation, weigher, precision=HIGHEST)  29.1 us
  transfers between devices with their start and end apart: 2, of which 2 were waited for; matrix products, arithmetic and copies ran while one was open for 13% of the time, Pallas kernels for 0%

commit v1 on v0

v1 whole, which is shorter than its diff:
```python
import functools
import math

import jax
import jax.numpy as jnp
from jax import lax
from jax.experimental import pallas as pl
from jax.experimental.pallas import tpu as pltpu
from jax.sharding import PartitionSpec as P

NEG_FILL = -1e30
NEG_CLAMP = -1e29
SOFT_CAP = 10.0
HIGHEST = lax.Precision.HIGHEST
F32 = jnp.float32
BF16 = jnp.bfloat16
MESH = pl.DeviceIdType.MESH

USERS = 8
CAND_DEV = 512
EVENTS = 2048
WIDTH = 256
SHORT = 256
SCORE_H = 128
OWN = 16
BLOCKS = 32
OWN_ALL = USERS * OWN
CGROUP = 4
DELAY = (3, 5, 6, 7, 8)
GELU_K = math.sqrt(2.0 / math.pi)
GELU_C = 0.044715


def dot(a, b, ca=1, cb=0, precision=None):
    return lax.dot_general(
        a, b, (((ca,), (cb,)), ((), ())), precision=precision, preferred_element_type=F32
    )


def gelu(p):
    return 0.5 * p * (1.0 + jnp.tanh(GELU_K * (p + GELU_C * p * p * p)))


def diag_row(col, n=128):
    lane = lax.broadcasted_iota(jnp.int32, (n, n), 1)
    sub = lax.broadcasted_iota(jnp.int32, (n, n), 0)
    return jnp.sum(jnp.where(lane == sub, jnp.broadcast_to(col, (n, n)), 0.0), axis=0, keepdims=True)


def to_column(row):
    return jnp.transpose(jnp.broadcast_to(row, (128, 128)))


def main_kernel(
    lengths,
    history,
    candidates,
    short,
    pad_mask,
    short_mask,
    query_gain,
    value_weight,
    head_weight,
    head_vector,
    pair_weight,
    event_weight,
    scoring_bias,
    weigher,
    pooling_weight,
    itemwise_weight,
    hidden_bias,
    output_vector,
    logits_out,
    grads_out,
    small_out,
    hist,
    qs,
    scores,
    probs,
    inv_col,
    lse_col,
    acc,
    lse,
    rv0,
    rv1,
    rv2,
    rv3,
    rv4,
    rl,
    oc,
    pw_t,
    ew_t,
    w_full,
    b_full,
    wb,
    pre,
    att,
    interest,
    datt,
    pg,
    mtot,
    msum,
    eg,
    rows_t,
    dh,
    mlp,
    st1,
    st2,
    sm1,
    sm2,
    gb,
    r0,
    r1,
    r2,
    hist_sem,
    rs_vs,
    rs_vr,
    rs_ls,
    rs_lr,
    st1_s,
    st1_r,
    st2_s,
    st2_r,
    sm1_s,
    sm1_r,
    sm2_s,
    sm2_r,
    a0_s,
    a0_r,
    a1_s,
    a1_r,
    a2_s,
    a2_r,
    a3_s,
    a3_r,
    a4_s,
    a4_r,
):
    rv = (rv0, rv1, rv2, rv3, rv4)
    cand = lax.axis_index("cand")
    ctx = lax.axis_index("ctx")
    x = ctx % 4
    y_hi = (ctx // 4) % 2
    z = ctx // 8
    y_lo = cand // 2
    core = cand % 2
    y = y_hi * 2 + y_lo
    place8 = y_hi * 4 + cand
    place16 = z * 4 + x

    def peer8(k):
        return (k % 4, z * 8 + (k // 4) * 4 + x)

    def peer16(k):
        return (cand, (k // 4) * 8 + y_hi * 4 + k % 4)

    def peer_y(k):
        return ((k % 2) * 2 + core, z * 8 + (k // 2) * 4 + x)

    sibling = (y_lo * 2 + 1 - core, ctx)

    def hist_copy(u):
        return pltpu.make_async_copy(history.at[u], hist.at[u], hist_sem.at[u])

    barrier = pltpu.get_barrier_semaphore()
    for d in range(1, 8):
        pl.semaphore_signal(barrier, inc=1, device_id=peer8((place8 + d) % 8), device_id_type=MESH)
    for d in range(1, 16):
        pl.semaphore_signal(
            barrier, inc=1, device_id=peer16((place16 + d) % 16), device_id_type=MESH
        )
    for u in range(USERS):
        hist_copy(u).start()

    pw_t[...] = jnp.transpose(pair_weight[...])
    ew_t[...] = jnp.transpose(event_weight[...])
    wc = to_column(weigher[...])
    bc = to_column(scoring_bias[...])
    w_full[:, :128] = wc
    w_full[:, 128:] = wc
    b_full[:, :128] = bc
    b_full[:, 128:] = bc
    for u in range(USERS):
        oc[u] = candidates[u, pl.ds(pl.multiple_of(ctx * OWN, OWN), OWN), :].astype(F32)
    pg[...] = jnp.zeros_like(pg)
    mtot[...] = jnp.zeros_like(mtot)
    eg[...] = jnp.zeros_like(eg)

    stride1 = 1 + 7 * core
    stride2 = 8 - 7 * core
    c1 = (ctx // stride1) % 4
    c2 = (ctx // stride2) % 4

    def bits_of(c):
        low, high = c % 2, c // 2
        return low + high - 2 * low * high, high

    def rs_plan(k, u):
        q = u % 2
        a1, b1 = bits_of(c1)
        a2, b2 = bits_of(c2)
        bits = (a1 + q * (b1 - a1), b1 + q * (a1 - b1), a2 + q * (b2 - a2), b2 + q * (a2 - b2), y_hi)
        start = 0
        for j in range(k):
            start = start + bits[j] * (16 >> j)
        n = 16 >> k
        keep = start + bits[k] * n
        send = start + (1 - bits[k]) * n
        if k == 4:
            partner = ctx + (1 - 2 * y_hi) * 4
        else:
            c, stride = (c1, stride1) if k < 2 else (c2, stride2)
            pa = c + 1 - 2 * (c % 2)
            pb = 3 - c
            pc = pa + q * (pb - pa) if k % 2 == 0 else pb + q * (pa - pb)
            partner = ctx + (pc - c) * stride
        return (cand, partner), keep, send

    def rs_copies(k, u):
        device, _, send = rs_plan(k, u)
        n = 16 >> k
        value = pltpu.make_async_remote_copy(
            src_ref=acc.at[u, pl.ds(send, n)],
            dst_ref=rv[k].at[u],
            send_sem=rs_vs.at[k, u],
            recv_sem=rs_vr.at[k, u],
            device_id=device,
            device_id_type=MESH,
        )
        if k == 0:
            src, dst = lse.at[k, u, pl.ds(send // 8, 2)], rl.at[u, pl.ds(0, 2)]
        else:
            src, dst = lse.at[k, u, pl.ds(send // 8, 1)], rl.at[u, pl.ds(1 + k, 1)]
        weight = pltpu.make_async_remote_copy(
            src_ref=src,
            dst_ref=dst,
            send_sem=rs_ls.at[k, u],
            recv_sem=rs_lr.at[k, u],
            device_id=device,
            device_id_type=MESH,
        )
        return value, weight

    def rs_send(k, u):
        for copy in rs_copies(k, u):
            copy.start()

    def rs_merge(k, u):
        for copy in rs_copies(k, u):
            copy.wait()
        _, keep, _ = rs_plan(k, u)
        n = 16 >> k
        rows = 2 if k == 0 else 1
        per_row = min(n, 8)
        for r in range(rows):
            row = keep // 8 + r
            mine = lse[k, u, row]
            other = rl[u, (r if k == 0 else 1 + k)]
            top = jnp.maximum(mine, other)
            e_mine = jnp.exp(mine - top)
            e_other = jnp.exp(other - top)
            total = e_mine + e_other
            share = e_other / total
            if k < 4:
                lse[k + 1, u, row] = top + jnp.log(total)
            share16 = jnp.concatenate([share, share], axis=0)
            lane = lax.broadcasted_iota(jnp.int32, (16, 128), 1)
            sub = lax.broadcasted_iota(jnp.int32, (16, 128), 0)
            for b in range(per_row):
                at = keep + r * 8 + b
                off = (at % 8) * 16
                col = jnp.sum(
                    jnp.where(lane - sub == off, share16, 0.0), axis=1, keepdims=True
                )
                own = acc[u, at]
                got = rv[k][u, r * 8 + b]
                acc[u, at] = own + col * (got - own)

    def teacher_user(u):
        q = u % 2
        gain = query_gain[...] * (1.0 / 16.0)
        for pos in range(BLOCKS):
            p4, p3, p2, p1, p0 = ((pos >> s) & 1 for s in (4, 3, 2, 1, 0))
            first = 2 * (p3 + q * (p4 - p3)) + (p4 ^ p3)
            second = 2 * (p1 + q * (p2 - p1)) + (p2 ^ p1)
            block = first * stride1 + second * stride2 + p0 * 4
            rows = candidates[u, pl.ds(pl.multiple_of(block * 16, 16), 16), :]
            qs[pos * 16 : pos * 16 + 16, :] = (rows.astype(F32) * gain).astype(BF16)
        spot = lax.broadcasted_iota(jnp.int32, (1, EVENTS), 1) + ctx * EVENTS
        ok = (spot < lengths[u]) & ((pad_mask[pl.ds(u, 1), :] == 1) | (spot == 0))
        bias = jnp.where(ok, 0.0, NEG_FILL)
        hist_copy(u).wait()
        for t in range(4):
            cols = slice(t * 512, t * 512 + 512)
            scores[:, cols] = dot(qs[...], hist[u, cols, :], 1, 1) + bias[:, cols]

        def soft(r, carry):
            rows = pl.ds(pl.multiple_of(r * 32, 32), 32)
            s = scores[rows, :]
            m = jnp.maximum(jnp.max(s, axis=1, keepdims=True), NEG_CLAMP)
            e = jnp.exp(s - m)
            total = jnp.sum(e, axis=1, keepdims=True)
            probs[rows, :] = e.astype(BF16)
            some = total > 0.0
            safe = jnp.where(some, total, 1.0)
            lse_col[rows, :] = jnp.broadcast_to(
                jnp.where(some, m + jnp.log(safe), NEG_FILL), (32, 128)
            )
            inv_col[rows, :] = jnp.broadcast_to(1.0 / safe, (32, 128))
            return carry

        lax.fori_loop(0, 16, soft, 0)
        lane = lax.broadcasted_iota(jnp.int32, (128, 128), 1)
        sub = lax.broadcasted_iota(jnp.int32, (128, 128), 0)
        for g in range(4):
            rows = slice(g * 128, g * 128 + 128)
            row = jnp.sum(jnp.where(lane == sub, lse_col[rows, :], 0.0), axis=0, keepdims=True)
            lse[0, u, g] = jnp.broadcast_to(row, (8, 128))
        for t in range(2):
            rows = slice(t * 256, t * 256 + 256)
            out = dot(probs[rows, :], hist[u])
            inv = inv_col[rows, :]
            acc[u, t * 16 : t * 16 + 16, :, :128] = (out[:, :128] * inv).reshape(16, 16, 128)
            acc[u, t * 16 : t * 16 + 16, :, 128:] = (out[:, 128:] * inv).reshape(16, 16, 128)

    def short_ok(u):
        spot = lax.broadcasted_iota(jnp.int32, (1, SHORT), 1)
        return (short_mask[pl.ds(u, 1), :] == 1) | (spot == 0)

    def student_user(u):
        def group(cg, carry):
            for j in range(CGROUP):
                c = cg * CGROUP + j
                w = pw_t[...] * oc[u, pl.ds(c, 1), :] + ew_t[...]
                high = w.astype(BF16)
                wb[0, j * 128 : j * 128 + 128, :] = high
                wb[1, j * 128 : j * 128 + 128, :] = (w - high.astype(F32)).astype(BF16)
            p = dot(wb[0], short[u], 1, 1) + dot(wb[1], short[u], 1, 1)
            for j in range(CGROUP):
                c = cg * CGROUP + j
                pj = p[j * 128 : j * 128 + 128, :] + b_full[...]
                pre[u, c] = pj
                att[u, pl.ds(c, 1), :] = jnp.sum(
                    jnp.maximum(pj, 0.0) * w_full[...], axis=0, keepdims=True
                )
            return carry

        lax.fori_loop(0, OWN // CGROUP, group, 0)
        weights = jnp.where(short_ok(u), att[u], 0.0)
        interest[u] = dot(weights, short[u].astype(F32), 1, 0, HIGHEST)

    pl.semaphore_wait(barrier, 22)

    def teacher_slot(i, carry):
        teacher_user(i)
        rs_send(0, i)
        for k in reversed(range(5)):

            @pl.when(i >= DELAY[k])
            def _(k=k):
                rs_merge(k, i - DELAY[k])
                if k < 4:
                    rs_send(k + 1, i - DELAY[k])

        return carry

    lax.fori_loop(0, USERS, teacher_slot, 0)

    def student_slot(i, carry):
        student_user(i - USERS)
        for k in reversed(range(5)):

            @pl.when(i - DELAY[k] < USERS)
            def _(k=k):
                rs_merge(k, i - DELAY[k])
                if k < 4:
                    rs_send(k + 1, i - DELAY[k])

        return carry

    lax.fori_loop(USERS, 2 * USERS, student_slot, 0)

    own_all = oc[...].reshape(OWN_ALL, WIDTH)
    parts = []
    for u in range(USERS):
        _, keep, _ = rs_plan(4, u)
        parts.append(acc[u, keep])
    pooled = dot(jnp.concatenate(parts, axis=0), value_weight[...].astype(F32), 1, 0, HIGHEST)
    normed = pooled * lax.rsqrt(jnp.mean(pooled * pooled, axis=1, keepdims=True) + 1e-6)
    mixed = (normed * own_all).astype(BF16)
    t_hidden = gelu(dot(mixed, head_weight[...]))
    t_logit = SOFT_CAP * jnp.tanh(
        jnp.sum(t_hidden * head_vector[...], axis=1, keepdims=True) / SOFT_CAP
    )
    lane = lax.broadcasted_iota(jnp.int32, (OWN_ALL, 128), 1)
    sub = lax.broadcasted_iota(jnp.int32, (OWN_ALL, 128), 0)
    logits_out[...] = jnp.sum(
        jnp.where(lane == sub % OWN, jnp.broadcast_to(t_logit, (OWN_ALL, 128)), 0.0).reshape(
            USERS, OWN, 128
        ),
        axis=1,
    )

    inter = interest[...].reshape(OWN_ALL, WIDTH)
    hid = (
        dot(inter, pooling_weight[...], 1, 0, HIGHEST)
        + dot(own_all, itemwise_weight[...], 1, 0, HIGHEST)
        + hidden_bias[...]
    )
    th = jnp.tanh(GELU_K * (hid + GELU_C * hid * hid * hid))
    s_hidden = 0.5 * hid * (1.0 + th)
    slope = 0.5 * (1.0 + th) + 0.5 * hid * (1.0 - th * th) * (
        GELU_K * (1.0 + 3.0 * GELU_C * hid * hid)
    )
    s_tanh = jnp.tanh(
        jnp.sum(s_hidden * output_vector[...], axis=1, keepdims=True) / SOFT_CAP
    )
    s_logit = SOFT_CAP * s_tanh

    s_exp = jnp.broadcast_to(jnp.exp(s_logit), (OWN_ALL, 128))
    t_exp = jnp.broadcast_to(jnp.exp(t_logit), (OWN_ALL, 128))

    def exchange(slots, count, me, peer, send_sem, recv_sem):
        def copy(k, to):
            return pltpu.make_async_remote_copy(
                src_ref=slots.at[me],
                dst_ref=slots.at[me],
                send_sem=send_sem.at[k],
                recv_sem=recv_sem.at[me],
                device_id=to,
                device_id_type=MESH,
            )

        def arrival(k):
            return pltpu.make_async_remote_copy(
                src_ref=slots.at[me],
                dst_ref=slots.at[k],
                send_sem=send_sem.at[k],
                recv_sem=recv_sem.at[k],
                device_id=peer(k),
                device_id_type=MESH,
            )

        def start():
            for d in range(1, count):
                k = (me + d) % count
                copy(k, peer(k)).start()

        def wait():
            for d in range(1, count):
                k = (me + d) % count
                arrival(k).wait_recv()
            for d in range(1, count):
                k = (me + d) % count
                copy(k, peer(k)).wait_send()

        return start, wait

    rows_t[0] = jnp.transpose(inter)
    rows_t[1] = jnp.transpose(own_all)
    st1[place8, 0] = jnp.sum(s_exp.reshape(USERS, OWN, 128), axis=1)
    st1[place8, 1] = jnp.sum(t_exp.reshape(USERS, OWN, 128), axis=1)
    start, wait = exchange(st1, 8, place8, peer8, st1_s, st1_r)
    start()
    wait()
    st2[place16] = jnp.sum(st1[...], axis=0)
    start, wait = exchange(st2, 16, place16, peer16, st2_s, st2_r)
    start()
    wait()
    sums = jnp.sum(st2[...], axis=0)

    def wide(v):
        return jnp.broadcast_to(v[:, None, :], (USERS, OWN, 128)).reshape(OWN_ALL, 128)

    scale = math.sqrt(4 * CAND_DEV / USERS)
    logit_grad = scale * (s_exp / wide(sums[0]) - t_exp / wide(sums[1]))
    draw = logit_grad[:, :1] * (1.0 - s_tanh * s_tanh)
    dhid = draw * output_vector[...] * slope
    hidden_grad = jnp.sum(dhid, axis=0, keepdims=True)
    output_grad = jnp.sum(s_hidden * draw, axis=0, keepdims=True)
    dh[...] = dhid
    dinter = dot(dhid, pooling_weight[...], 1, 1, HIGHEST)
    for u in range(USERS):
        d = dot(dinter[u * OWN : u * OWN + OWN, :], short[u].astype(F32), 1, 1, HIGHEST)
        datt[u] = jnp.where(short_ok(u), d, 0.0)

    def mlp_half(h, carry):
        mlp[h] = dot(rows_t[h], dh[...], 1, 0, HIGHEST)
        return carry

    lax.fori_loop(0, 2, mlp_half, 0)

    def back_user(u, carry):
        msum[...] = jnp.zeros_like(msum)

        def group(cg, inner):
            total = msum[...]
            for j in range(CGROUP):
                c = cg * CGROUP + j
                m = jnp.where(pre[u, c] > 0.0, datt[u, pl.ds(c, 1), :], 0.0)
                total = total + m
                wb[0, j * 128 : j * 128 + 128, :] = m.astype(BF16)
            msum[...] = total
            g = dot(wb[0], short[u])
            add = pg[...]
            for j in range(CGROUP):
                c = cg * CGROUP + j
                add = add + g[j * 128 : j * 128 + 128, :] * oc[u, pl.ds(c, 1), :]
            pg[...] = add
            return inner

        lax.fori_loop(0, OWN // CGROUP, group, 0)
        mtot[...] += msum[...]
        eg[...] += dot(msum[...], short[u].astype(F32), 1, 0, HIGHEST)
        return carry

    lax.fori_loop(0, USERS, back_user, 0)

    g_row = diag_row(jnp.sum(mtot[...], axis=1, keepdims=True))
    sm1[place8] = jnp.concatenate(
        [
            jnp.concatenate([g_row, jnp.zeros_like(g_row)], axis=1),
            hidden_grad,
            output_grad,
            jnp.zeros((5, WIDTH), F32),
        ],
        axis=0,
    )
    small_start, small_wait = exchange(sm1, 8, place8, peer8, sm1_s, sm1_r)
    small_start()

    def put(first, value):
        for c in range(value.shape[0] // 8):
            at = first // 8 + c
            half, rest = divmod(at, 48)
            gb[half, rest // 3, (rest % 3) * 8 : (rest % 3) * 8 + 8, :] = value[c * 8 : c * 8 + 8, :]

    put(0, pg[...])
    put(128, eg[...])
    put(256, mlp[0])
    put(512, mlp[1])

    swap = pltpu.make_async_remote_copy(
        src_ref=gb.at[1 - core],
        dst_ref=r0,
        send_sem=a0_s,
        recv_sem=a0_r,
        device_id=sibling,
        device_id_type=MESH,
    )
    swap.start()
    small_wait()
    sm2[place16] = jnp.sum(sm1[...], axis=0)
    small_start, small_wait = exchange(sm2, 16, place16, peer16, sm2_s, sm2_r)
    small_start()
    swap.wait()
    r0[...] = r0[...] + gb[core]

    def scatter(k, slot):
        return pltpu.make_async_remote_copy(
            src_ref=r0.at[k],
            dst_ref=r1.at[slot],
            send_sem=a1_s.at[k],
            recv_sem=a1_r.at[slot],
            device_id=peer16(k),
            device_id_type=MESH,
        )

    others = [(place16 + d) % 16 for d in range(1, 16)]
    for k in others:
        scatter(k, place16).start()
    r1[place16] = r0[place16]
    for k in others:
        scatter(k, k).wait_recv()
    r2[y] = jnp.sum(r1[...], axis=0)
    start, wait = exchange(r2, 4, y, peer_y, a2_s, a2_r)
    start()
    wait()
    grads_out[core, place16] = jnp.sum(r2[...], axis=0)

    def spread(k, slot):
        return pltpu.make_async_remote_copy(
            src_ref=grads_out.at[core, slot],
            dst_ref=grads_out.at[core, slot],
            send_sem=a3_s.at[k],
            recv_sem=a3_r.at[slot],
            device_id=peer16(k),
            device_id_type=MESH,
        )

    for k in others:
        spread(k, place16).start()
    for k in others:
        scatter(k, place16).wait_send()
    small_wait()
    small_out[...] = jnp.sum(sm2[...], axis=0)
    for k in others:
        spread(k, k).wait_recv()
    last = pltpu.make_async_remote_copy(
        src_ref=grads_out.at[core],
        dst_ref=grads_out.at[core],
        send_sem=a4_s,
        recv_sem=a4_r,
        device_id=sibling,
        device_id_type=MESH,
    )
    last.start()
    for k in others:
        spread(k, place16).wait_send()
    last.wait_send()
    pltpu.make_async_remote_copy(
        src_ref=grads_out.at[core],
        dst_ref=grads_out.at[1 - core],
        send_sem=a4_s,
        recv_sem=a4_r,
        device_id=sibling,
        device_id_type=MESH,
    ).wait_recv()


def finish_kernel(
    logits,
    grads,
    small,
    pair_weight,
    event_weight,
    scoring_bias,
    weigher,
    logits_out,
    pair_out,
    event_out,
    scoring_out,
    weigher_out,
    pooling_out,
    itemwise_out,
    hidden_out,
    output_out,
):
    flat = grads[...].reshape(768, WIDTH)
    w = weigher[...]
    pair = jnp.transpose(flat[:128])
    event = jnp.transpose(flat[128:256])
    g = small[0:1, :128]
    pair_out[...] = pair * w
    event_out[...] = event * w
    scoring_out[...] = g * w
    weigher_out[...] = scoring_bias[...] * g + jnp.sum(
        pair * pair_weight[...] + event * event_weight[...], axis=0, keepdims=True
    )
    pooling_out[...] = flat[256:512]
    itemwise_out[...] = flat[512:768]
    hidden_out[...] = small[1:2, :]
    output_out[...] = small[2:3, :]
    logits_out[...] = logits[:, :OWN]


def body(
    history,
    candidates,
    short_hist,
    lengths,
    pad_mask,
    short_mask,
    query_gain,
    value_weight,
    head_weight,
    head_vector,
    pair_weight,
    event_weight,
    scoring_bias,
    weigher,
    pooling_weight,
    itemwise_weight,
    hidden_bias,
    output_vector,
):
    vmem = pl.BlockSpec(memory_space=pltpu.VMEM)
    row = lambda v: v.reshape(1, -1)
    dma = pltpu.SemaphoreType.DMA
    logits, grads, small = pl.pallas_call(
        main_kernel,
        out_shape=(
            jax.ShapeDtypeStruct((USERS, 128), F32),
            jax.ShapeDtypeStruct((2, 16, 24, WIDTH), F32),
            jax.ShapeDtypeStruct((8, WIDTH), F32),
        ),
        in_specs=[
            pl.BlockSpec(memory_space=pltpu.SMEM),
            pl.BlockSpec(memory_space=pl.ANY),
        ]
        + [vmem] * 16,
        out_specs=(vmem, vmem, vmem),
        scratch_shapes=[
            pltpu.VMEM((USERS, EVENTS, WIDTH), BF16),
            pltpu.VMEM((CAND_DEV, WIDTH), BF16),
            pltpu.VMEM((CAND_DEV, EVENTS), F32),
            pltpu.VMEM((CAND_DEV, EVENTS), BF16),
            pltpu.VMEM((CAND_DEV, 128), F32),
            pltpu.VMEM((CAND_DEV, 128), F32),
            pltpu.VMEM((USERS, BLOCKS, OWN, WIDTH), F32),
            pltpu.VMEM((5, USERS, 4, 8, 128), F32),
            pltpu.VMEM((USERS, 16, OWN, WIDTH), F32),
            pltpu.VMEM((USERS, 8, OWN, WIDTH), F32),
            pltpu.VMEM((USERS, 4, OWN, WIDTH), F32),
            pltpu.VMEM((USERS, 2, OWN, WIDTH), F32),
            pltpu.VMEM((USERS, 1, OWN, WIDTH), F32),
            pltpu.VMEM((USERS, 6, 8, 128), F32),
            pltpu.VMEM((USERS, OWN, WIDTH), F32),
            pltpu.VMEM((SCORE_H, WIDTH), F32),
            pltpu.VMEM((SCORE_H, WIDTH), F32),
            pltpu.VMEM((SCORE_H, WIDTH), F32),
            pltpu.VMEM((SCORE_H, WIDTH), F32),
            pltpu.VMEM((2, CGROUP * SCORE_H, WIDTH), BF16),
            pltpu.VMEM((USERS, OWN, SCORE_H, SHORT), F32),
            pltpu.VMEM((USERS, OWN, SHORT), F32),
            pltpu.VMEM((USERS, OWN, WIDTH), F32),
            pltpu.VMEM((USERS, OWN, SHORT), F32),
            pltpu.VMEM((SCORE_H, WIDTH), F32),
            pltpu.VMEM((SCORE_H, SHORT), F32),
            pltpu.VMEM((SCORE_H, SHORT), F32),
            pltpu.VMEM((SCORE_H, WIDTH), F32),
            pltpu.VMEM((2, WIDTH, OWN_ALL), F32),
            pltpu.VMEM((OWN_ALL, WIDTH), F32),
            pltpu.VMEM((2, WIDTH, WIDTH), F32),
            pltpu.VMEM((8, 2, USERS, 128), F32),
            pltpu.VMEM((16, 2, USERS, 128), F32),
            pltpu.VMEM((8, 8, WIDTH), F32),
            pltpu.VMEM((16, 8, WIDTH), F32),
            pltpu.VMEM((2, 16, 24, WIDTH), F32),
            pltpu.VMEM((16, 24, WIDTH), F32),
            pltpu.VMEM((16, 24, WIDTH), F32),
            pltpu.VMEM((4, 24, WIDTH), F32),
            dma((USERS,)),
            dma((5, USERS)),
            dma((5, USERS)),
            dma((5, USERS)),
            dma((5, USERS)),
            dma((8,)),
            dma((8,)),
            dma((16,)),
            dma((16,)),
            dma((8,)),
            dma((8,)),
            dma((16,)),
            dma((16,)),
            dma,
            dma,
            dma((16,)),
            dma((16,)),
            dma((4,)),
            dma((4,)),
            dma((16,)),
            dma((16,)),
            dma,
            dma,
        ],
        compiler_params=pltpu.CompilerParams(
            collective_id=0, has_side_effects=True, vmem_limit_bytes=62 * 1024 * 1024
        ),
        name="main_kernel",
    )(
        lengths,
        history,
        candidates,
        short_hist,
        pad_mask,
        short_mask,
        row(query_gain),
        value_weight,
        head_weight,
        row(head_vector),
        pair_weight,
        event_weight,
        row(scoring_bias),
        row(weigher),
        pooling_weight,
        itemwise_weight,
        row(hidden_bias),
        row(output_vector),
    )
    out = pl.pallas_call(
        finish_kernel,
        out_shape=(
            jax.ShapeDtypeStruct((USERS, OWN), F32),
            jax.ShapeDtypeStruct((WIDTH, SCORE_H), F32),
            jax.ShapeDtypeStruct((WIDTH, SCORE_H), F32),
            jax.ShapeDtypeStruct((1, SCORE_H), F32),
            jax.ShapeDtypeStruct((1, SCORE_H), F32),
            jax.ShapeDtypeStruct((WIDTH, WIDTH), F32),
            jax.ShapeDtypeStruct((WIDTH, WIDTH), F32),
            jax.ShapeDtypeStruct((1, WIDTH), F32),
            jax.ShapeDtypeStruct((1, WIDTH), F32),
        ),
        in_specs=[vmem] * 7,
        out_specs=(vmem,) * 9,
        name="finish_kernel",
    )(logits, grads, small, pair_weight, event_weight, row(scoring_bias), row(weigher))
    flat = lambda v: v.reshape(-1)
    return (
        out[0],
        out[1],
        out[2],
        flat(out[3]),
        flat(out[4]),
        out[5],
        out[6],
        flat(out[7]),
        flat(out[8]),
    )


def solution(mesh):
    placed = (P(None, "ctx", None), P(None, "cand", None), P(), P(), P(None, "ctx")) + (P(),) * 13
    return jax.shard_map(
        body,
        mesh=mesh,
        in_specs=placed,
        out_specs=(P(None, ("cand", "ctx")),) + (P(),) * 8,
        check_vma=False,
    )
```

time: 886 us -> 139 us (0.16)
  blocking collectives: 459 us -> 0 us
  matrix products: 179 us -> 0 us
  waiting for transfers between devices: 177 us -> 0 us
  Pallas kernels: 0 us -> 138 us
  other arithmetic: 35.5 us -> 0 us
  between operations: 14.7 us -> 0.66 us
  local copies, waits for them, and re-layouts: 14 us -> 0 us
    psum x3 -> x0, blocking collectives: 302 us -> none  [the longest x1 152 us: body(): lax.psum((block_total * factor, block_value * factor[:, :, None]), 'ctx')]
    dot_general x18 -> x0, matrix products: 179 us -> none  [the longest x2 105 us: student(): jnp.einsum('urse,ea->ursa', pairs, pair_weight, precision=HIGHEST)]
    psum x2 -> x0, waiting for transfers between devices: 177 us -> none  [the longest x1 110 us: body(): lax.psum((block_total * factor, block_value * factor[:, :, None]), 'ctx')]
    pmax x1 -> x0, blocking collectives: 158 us -> none  [body(): highest = lax.pmax(block_max, 'ctx')]
    pallas_call x0 -> x2, Pallas kernels: none -> 138 us  [the longest x1 136 us: body(): pl.pallas_call(main_kernel, out_shape=(jax.ShapeDtypeStruct((USERS, 128),...]
    reduce_sum x5 -> x0, other arithmetic: 21 us -> none  [the longest x1 14.6 us: body(): block_total = jnp.sum(block_exp, axis=2)]
    unnamed x32 -> x0, local copies, waits for them, and re-layouts: 12.3 us -> none
  transfers between devices with their start and end apart: 2 -> 0, of which waited for: 2 -> 0; matrix products, arithmetic and copies ran while one was open for 13% -> 0% of each run, Pallas kernels for 0% -> 0%
where the time goes in v1:
time: 139 us; the launch traced here: 138 us
  Pallas kernels  138 us (99%)
    pallas_call x1, Pallas kernels, body(): pl.pallas_call(main_kernel, out_shape=(jax.ShapeDtypeStruct((USERS, 128),...  136 us

profile of v1, /device:TPU:1, one launch (start us, length us, event | category | flops | bytes accessed | tf_op | source)
XLA Modules:
  0.0 138.4 jit_solution(6668503987098419922)
XLA Ops:
  0.6 135.6 %main_kernel.1 = (f32[8,128]{1,0:T(8,128)}, f32[2,16,24,256]{3,2,1,0:T(8,128)}, f32[8,256]{1,0:T(8,128)}) custom-call(s32[8]{0:T(128)} %lengths.1, bf16[8,2048,256]{2,1,0:T(8,128)(2,1)} %history.1, bf16[8,512,256]{2,1,0:T(8,128)(2,1)} %candidates.1, bf16[8,256,256]{2,1,0:T(8,128)(2,1)} %short.1, s32[8,2048]{1,0:T(8,128)} %pad_mask.1, s32[8,256]{1,0:T(8,128)} %short_mask.1, ...), custom_call_target="tpu_custom_call" | custom-call | tf_op jit(solution)/shard_map/main_kernel/pallas_call | solution.py:680
  136.2 2.2 %finish_kernel.1 = (f32[8,16]{1,0:T(8,128)}, f32[256,128]{1,0:T(8,128)}, f32[256,128]{1,0:T(8,128)}, f32[1,128]{1,0:T(1,128)}, f32[1,128]{1,0:T(1,128)}, /*index...) custom-call(f32[8,128]{1,0:T(8,128)} %get-tuple-element.21.logits, ...), custom_call_target="tpu_custom_call" | custom-call | tf_op jit(solution)/shard_map/finish_kernel/pallas_call | solution.py:781

commit v2 on v1

--- a/solution.py
+++ b/solution.py
@@ -26,7 +26,8 @@
 BLOCKS = 32
 OWN_ALL = USERS * OWN
 CGROUP = 4
-DELAY = (3, 5, 6, 7, 8)
+DELAY = (3, 5, 7, 9, 11)
+SLOTS = USERS + DELAY[4]
 GELU_K = math.sqrt(2.0 / math.pi)
 GELU_C = 0.044715
 
@@ -54,31 +55,43 @@
 def main_kernel(
     lengths,
     history,
-    candidates,
-    short,
+    candidates_hbm,
+    short_hbm,
+    value_hbm,
+    head_hbm,
+    pair_hbm,
+    event_hbm,
+    pooling_hbm,
+    itemwise_hbm,
     pad_mask,
     short_mask,
     query_gain,
-    value_weight,
-    head_weight,
     head_vector,
-    pair_weight,
-    event_weight,
     scoring_bias,
     weigher,
-    pooling_weight,
-    itemwise_weight,
     hidden_bias,
     output_vector,
     logits_out,
-    grads_out,
+    mlp_out,
+    att_out,
     small_out,
     hist,
+    candidates,
+    short,
+    value_weight,
+    head_weight,
+    pair_weight,
+    event_weight,
+    pooling_weight,
+    itemwise_weight,
     qs,
     scores,
     probs,
     inv_col,
     lse_col,
+    top_part,
+    top_col,
+    sum_part,
     acc,
     lse,
     rv0,
@@ -97,10 +110,10 @@
     att,
     interest,
     datt,
-    pg,
-    mtot,
-    msum,
-    eg,
+    exps,
+    unit_sums,
+    row_scale,
+    cand_scale,
     rows_t,
     dh,
     mlp,
@@ -108,11 +121,17 @@
     st2,
     sm1,
     sm2,
-    gb,
-    r0,
-    r1,
-    r2,
+    gb0,
+    gb1,
+    r00,
+    r01,
+    r10,
+    r11,
+    r20,
+    r21,
     hist_sem,
+    cand_sem,
+    load_sem,
     rs_vs,
     rs_vr,
     rs_ls,
@@ -136,6 +155,15 @@
     a4_s,
     a4_r,
 ):
+    loads = (
+        (short_hbm, short),
+        (pair_hbm, pair_weight),
+        (event_hbm, event_weight),
+        (pooling_hbm, pooling_weight),
+        (itemwise_hbm, itemwise_weight),
+        (value_hbm, value_weight),
+        (head_hbm, head_weight),
+    )
     rv = (rv0, rv1, rv2, rv3, rv4)
     cand = lax.axis_index("cand")
     ctx = lax.axis_index("ctx")
@@ -162,6 +190,12 @@
     def hist_copy(u):
         return pltpu.make_async_copy(history.at[u], hist.at[u], hist_sem.at[u])
 
+    def cand_copy(u):
+        return pltpu.make_async_copy(candidates_hbm.at[u], candidates.at[u], cand_sem.at[u])
+
+    def load(k):
+        return pltpu.make_async_copy(loads[k][0], loads[k][1], load_sem.at[k])
+
     barrier = pltpu.get_barrier_semaphore()
     for d in range(1, 8):
         pl.semaphore_signal(barrier, inc=1, device_id=peer8((place8 + d) % 8), device_id_type=MESH)
@@ -170,21 +204,25 @@
             barrier, inc=1, device_id=peer16((place16 + d) % 16), device_id_type=MESH
         )
     for u in range(USERS):
+        cand_copy(u).start()
         hist_copy(u).start()
-
-    pw_t[...] = jnp.transpose(pair_weight[...])
-    ew_t[...] = jnp.transpose(event_weight[...])
-    wc = to_column(weigher[...])
-    bc = to_column(scoring_bias[...])
-    w_full[:, :128] = wc
-    w_full[:, 128:] = wc
-    b_full[:, :128] = bc
-    b_full[:, 128:] = bc
-    for u in range(USERS):
-        oc[u] = candidates[u, pl.ds(pl.multiple_of(ctx * OWN, OWN), OWN), :].astype(F32)
-    pg[...] = jnp.zeros_like(pg)
-    mtot[...] = jnp.zeros_like(mtot)
-    eg[...] = jnp.zeros_like(eg)
+    for k in range(len(loads)):
+        load(k).start()
+
+    def set_up():
+        for k in range(len(loads)):
+            load(k).wait()
+        pw_t[...] = jnp.transpose(pair_weight[...])
+        ew_t[...] = jnp.transpose(event_weight[...])
+        wc = to_column(weigher[...])
+        bc = to_column(scoring_bias[...])
+        w_full[:, :128] = wc
+        w_full[:, 128:] = wc
+        b_full[:, :128] = bc
+        b_full[:, 128:] = bc
+        for u in range(USERS):
+            oc[u] = candidates[u, pl.ds(pl.multiple_of(ctx * OWN, OWN), OWN), :].astype(F32)
+        unit_sums[...] = jnp.zeros_like(unit_sums)
 
     stride1 = 1 + 7 * core
     stride2 = 8 - 7 * core
@@ -279,6 +317,7 @@
     def teacher_user(u):
         q = u % 2
         gain = query_gain[...] * (1.0 / 16.0)
+        cand_copy(u).wait()
         for pos in range(BLOCKS):
             p4, p3, p2, p1, p0 = ((pos >> s) & 1 for s in (4, 3, 2, 1, 0))
             first = 2 * (p3 + q * (p4 - p3)) + (p4 ^ p3)
@@ -292,24 +331,29 @@
         hist_copy(u).wait()
         for t in range(4):
             cols = slice(t * 512, t * 512 + 512)
-            scores[:, cols] = dot(qs[...], hist[u, cols, :], 1, 1) + bias[:, cols]
-
-        def soft(r, carry):
-            rows = pl.ds(pl.multiple_of(r * 32, 32), 32)
-            s = scores[rows, :]
-            m = jnp.maximum(jnp.max(s, axis=1, keepdims=True), NEG_CLAMP)
-            e = jnp.exp(s - m)
-            total = jnp.sum(e, axis=1, keepdims=True)
-            probs[rows, :] = e.astype(BF16)
-            some = total > 0.0
-            safe = jnp.where(some, total, 1.0)
-            lse_col[rows, :] = jnp.broadcast_to(
-                jnp.where(some, m + jnp.log(safe), NEG_FILL), (32, 128)
-            )
-            inv_col[rows, :] = jnp.broadcast_to(1.0 / safe, (32, 128))
-            return carry
-
-        lax.fori_loop(0, 16, soft, 0)
+            s = dot(qs[...], hist[u, cols, :], 1, 1) + bias[:, cols]
+            scores[:, cols] = s
+            top = s[:, :128]
+            for g in range(1, 4):
+                top = jnp.maximum(top, s[:, g * 128 : g * 128 + 128])
+            top_part[...] = top if t == 0 else jnp.maximum(top_part[...], top)
+        top = jnp.maximum(jnp.max(top_part[...], axis=1, keepdims=True), NEG_CLAMP)
+        top_col[...] = jnp.broadcast_to(top, (CAND_DEV, 128))
+        for r in range(16):
+            rows = slice(r * 32, r * 32 + 32)
+            m = top_col[rows, :]
+            total = None
+            for g in range(16):
+                cols = slice(g * 128, g * 128 + 128)
+                e = jnp.exp(scores[rows, cols] - m)
+                probs[rows, cols] = e.astype(BF16)
+                total = e if total is None else total + e
+            sum_part[rows, :] = total
+        total = jnp.sum(sum_part[...], axis=1, keepdims=True)
+        some = total > 0.0
+        safe = jnp.where(some, total, 1.0)
+        lse_col[...] = jnp.where(some, top_col[...] + jnp.log(safe), NEG_FILL)
+        inv_col[...] = jnp.broadcast_to(1.0 / safe, (CAND_DEV, 128))
         lane = lax.broadcasted_iota(jnp.int32, (128, 128), 1)
         sub = lax.broadcasted_iota(jnp.int32, (128, 128), 0)
         for g in range(4):
@@ -328,14 +372,14 @@
         return (short_mask[pl.ds(u, 1), :] == 1) | (spot == 0)
 
     def student_user(u):
-        def group(cg, carry):
+        for cg in range(OWN // CGROUP):
             for j in range(CGROUP):
                 c = cg * CGROUP + j
                 w = pw_t[...] * oc[u, pl.ds(c, 1), :] + ew_t[...]
                 high = w.astype(BF16)
-                wb[0, j * 128 : j * 128 + 128, :] = high
-                wb[1, j * 128 : j * 128 + 128, :] = (w - high.astype(F32)).astype(BF16)
-            p = dot(wb[0], short[u], 1, 1) + dot(wb[1], short[u], 1, 1)
+                wb[cg, 0, j * 128 : j * 128 + 128, :] = high
+                wb[cg, 1, j * 128 : j * 128 + 128, :] = (w - high.astype(F32)).astype(BF16)
+            p = dot(wb[cg, 0], short[u], 1, 1) + dot(wb[cg, 1], short[u], 1, 1)
             for j in range(CGROUP):
                 c = cg * CGROUP + j
                 pj = p[j * 128 : j * 128 + 128, :] + b_full[...]
@@ -343,42 +387,90 @@
                 att[u, pl.ds(c, 1), :] = jnp.sum(
                     jnp.maximum(pj, 0.0) * w_full[...], axis=0, keepdims=True
                 )
-            return carry
-
-        lax.fori_loop(0, OWN // CGROUP, group, 0)
         weights = jnp.where(short_ok(u), att[u], 0.0)
         interest[u] = dot(weights, short[u].astype(F32), 1, 0, HIGHEST)
 
-    pl.semaphore_wait(barrier, 22)
+    def back_user(u):
+        for cg in range(OWN // CGROUP):
+            cols = []
+            for j in range(CGROUP):
+                c = cg * CGROUP + j
+                m = jnp.where(pre[u, c] > 0.0, datt[u, pl.ds(c, 1), :], 0.0)
+                wb[cg, 0, j * 128 : j * 128 + 128, :] = m.astype(BF16)
+                cols.append(jnp.sum(m, axis=1, keepdims=True))
+            g = dot(wb[cg, 0], short[u])
+            for j in range(CGROUP):
+                pre[u, cg * CGROUP + j] = g[j * 128 : j * 128 + 128, :]
+            lane = lax.broadcasted_iota(jnp.int32, (SCORE_H, OWN_ALL), 1)
+            units = unit_sums[...]
+            for j in range(CGROUP):
+                units = jnp.where(lane == u * OWN + cg * CGROUP + j, cols[j], units)
+            unit_sums[...] = units
+
+    def reduce_steps(i):
+        for k in reversed(range(5)):
+            u = i - DELAY[k]
+
+            def step(k=k, u=u):
+                rs_merge(k, u)
+                if k < 4:
+                    rs_send(k + 1, u)
+
+            pl.when((u >= 0) & (u < USERS))(step)
 
     def teacher_slot(i, carry):
         teacher_user(i)
+
+        @pl.when(i == 0)
+        def _():
+            pl.semaphore_wait(barrier, 22)
+
         rs_send(0, i)
-        for k in reversed(range(5)):
-
-            @pl.when(i >= DELAY[k])
-            def _(k=k):
-                rs_merge(k, i - DELAY[k])
-                if k < 4:
-                    rs_send(k + 1, i - DELAY[k])
-
+        reduce_steps(i)
         return carry
 
     lax.fori_loop(0, USERS, teacher_slot, 0)
+    set_up()
 
     def student_slot(i, carry):
         student_user(i - USERS)
-        for k in reversed(range(5)):
-
-            @pl.when(i - DELAY[k] < USERS)
-            def _(k=k):
-                rs_merge(k, i - DELAY[k])
-                if k < 4:
-                    rs_send(k + 1, i - DELAY[k])
-
+        reduce_steps(i)
         return carry
 
     lax.fori_loop(USERS, 2 * USERS, student_slot, 0)
+
+    own_all = oc[...].reshape(OWN_ALL, WIDTH)
+    inter = interest[...].reshape(OWN_ALL, WIDTH)
+    hid = (
+        dot(inter, pooling_weight[...], 1, 0, HIGHEST)
+        + dot(own_all, itemwise_weight[...], 1, 0, HIGHEST)
+        + hidden_bias[...]
+    )
+    th = jnp.tanh(GELU_K * (hid + GELU_C * hid * hid * hid))
+    s_hidden = 0.5 * hid * (1.0 + th)
+    slope = 0.5 * (1.0 + th) + 0.5 * hid * (1.0 - th * th) * (
+        GELU_K * (1.0 + 3.0 * GELU_C * hid * hid)
+    )
+    s_tanh = jnp.tanh(jnp.sum(s_hidden * output_vector[...], axis=1, keepdims=True) / SOFT_CAP)
+    draw = 1.0 - s_tanh * s_tanh
+    dhid = draw * output_vector[...] * slope
+    dinter = dot(dhid, pooling_weight[...], 1, 1, HIGHEST)
+    for u in range(USERS):
+        d = dot(dinter[u * OWN : u * OWN + OWN, :], short[u].astype(F32), 1, 1, HIGHEST)
+        datt[u] = jnp.where(short_ok(u), d, 0.0)
+    dh[0] = dhid
+    dh[1] = s_hidden * draw
+    s_exp = jnp.broadcast_to(jnp.exp(SOFT_CAP * s_tanh), (OWN_ALL, 128))
+    exps[0] = s_exp
+    rows_t[0] = jnp.transpose(inter)
+    rows_t[1] = jnp.transpose(own_all)
+
+    def back_slot(i, carry):
+        back_user(i - 2 * USERS)
+        reduce_steps(i)
+        return carry
+
+    lax.fori_loop(2 * USERS, SLOTS, back_slot, 0)
 
     own_all = oc[...].reshape(OWN_ALL, WIDTH)
     parts = []
@@ -401,24 +493,8 @@
         axis=1,
     )
 
-    inter = interest[...].reshape(OWN_ALL, WIDTH)
-    hid = (
-        dot(inter, pooling_weight[...], 1, 0, HIGHEST)
-        + dot(own_all, itemwise_weight[...], 1, 0, HIGHEST)
-        + hidden_bias[...]
-    )
-    th = jnp.tanh(GELU_K * (hid + GELU_C * hid * hid * hid))
-    s_hidden = 0.5 * hid * (1.0 + th)
-    slope = 0.5 * (1.0 + th) + 0.5 * hid * (1.0 - th * th) * (
-        GELU_K * (1.0 + 3.0 * GELU_C * hid * hid)
-    )
-    s_tanh = jnp.tanh(
-        jnp.sum(s_hidden * output_vector[...], axis=1, keepdims=True) / SOFT_CAP
-    )
-    s_logit = SOFT_CAP * s_tanh
-
-    s_exp = jnp.broadcast_to(jnp.exp(s_logit), (OWN_ALL, 128))
     t_exp = jnp.broadcast_to(jnp.exp(t_logit), (OWN_ALL, 128))
+    exps[1] = t_exp
 
     def exchange(slots, count, me, peer, send_sem, recv_sem):
         def copy(k, to):
@@ -456,16 +532,25 @@
 
         return start, wait
 
-    rows_t[0] = jnp.transpose(inter)
-    rows_t[1] = jnp.transpose(own_all)
-    st1[place8, 0] = jnp.sum(s_exp.reshape(USERS, OWN, 128), axis=1)
+    st1[place8, 0] = jnp.sum(exps[0].reshape(USERS, OWN, 128), axis=1)
     st1[place8, 1] = jnp.sum(t_exp.reshape(USERS, OWN, 128), axis=1)
+
+    def more_back(first, last):
+        def one(u, carry):
+            back_user(u)
+            return carry
+
+        lax.fori_loop(first, last, one, 0)
+
+    done = SLOTS - 2 * USERS
     start, wait = exchange(st1, 8, place8, peer8, st1_s, st1_r)
     start()
+    more_back(done, done + 3)
     wait()
     st2[place16] = jnp.sum(st1[...], axis=0)
     start, wait = exchange(st2, 16, place16, peer16, st2_s, st2_r)
     start()
+    more_back(done + 3, USERS)
     wait()
     sums = jnp.sum(st2[...], axis=0)
 
@@ -473,154 +558,160 @@
         return jnp.broadcast_to(v[:, None, :], (USERS, OWN, 128)).reshape(OWN_ALL, 128)
 
     scale = math.sqrt(4 * CAND_DEV / USERS)
-    logit_grad = scale * (s_exp / wide(sums[0]) - t_exp / wide(sums[1]))
-    draw = logit_grad[:, :1] * (1.0 - s_tanh * s_tanh)
-    dhid = draw * output_vector[...] * slope
-    hidden_grad = jnp.sum(dhid, axis=0, keepdims=True)
-    output_grad = jnp.sum(s_hidden * draw, axis=0, keepdims=True)
-    dh[...] = dhid
-    dinter = dot(dhid, pooling_weight[...], 1, 1, HIGHEST)
-    for u in range(USERS):
-        d = dot(dinter[u * OWN : u * OWN + OWN, :], short[u].astype(F32), 1, 1, HIGHEST)
-        datt[u] = jnp.where(short_ok(u), d, 0.0)
+    logit_grad = scale * (exps[0] / wide(sums[0]) - exps[1] / wide(sums[1]))
+    row_scale[:, :128] = logit_grad
+    row_scale[:, 128:] = logit_grad
+    cand_scale[...] = row_scale[...] * oc[...].reshape(OWN_ALL, WIDTH)
+    dh[0] = dh[0] * row_scale[...]
+    dh[1] = dh[1] * row_scale[...]
 
     def mlp_half(h, carry):
-        mlp[h] = dot(rows_t[h], dh[...], 1, 0, HIGHEST)
+        mlp[h] = dot(rows_t[h], dh[0], 1, 0, HIGHEST)
         return carry
 
     lax.fori_loop(0, 2, mlp_half, 0)
 
-    def back_user(u, carry):
-        msum[...] = jnp.zeros_like(msum)
-
-        def group(cg, inner):
-            total = msum[...]
-            for j in range(CGROUP):
-                c = cg * CGROUP + j
-                m = jnp.where(pre[u, c] > 0.0, datt[u, pl.ds(c, 1), :], 0.0)
-                total = total + m
-                wb[0, j * 128 : j * 128 + 128, :] = m.astype(BF16)
-            msum[...] = total
-            g = dot(wb[0], short[u])
-            add = pg[...]
-            for j in range(CGROUP):
-                c = cg * CGROUP + j
-                add = add + g[j * 128 : j * 128 + 128, :] * oc[u, pl.ds(c, 1), :]
-            pg[...] = add
-            return inner
-
-        lax.fori_loop(0, OWN // CGROUP, group, 0)
-        mtot[...] += msum[...]
-        eg[...] += dot(msum[...], short[u].astype(F32), 1, 0, HIGHEST)
-        return carry
-
-    lax.fori_loop(0, USERS, back_user, 0)
-
-    g_row = diag_row(jnp.sum(mtot[...], axis=1, keepdims=True))
+    others = [(place16 + d) % 16 for d in range(1, 16)]
+
+    def all_reduce(n, gb, r0, r1, r2, out):
+        def swap():
+            return pltpu.make_async_remote_copy(
+                src_ref=gb.at[1 - core],
+                dst_ref=r0,
+                send_sem=a0_s.at[n],
+                recv_sem=a0_r.at[n],
+                device_id=sibling,
+                device_id_type=MESH,
+            )
+
+        def scatter(k, slot):
+            return pltpu.make_async_remote_copy(
+                src_ref=r0.at[k],
+                dst_ref=r1.at[slot],
+                send_sem=a1_s.at[n, k],
+                recv_sem=a1_r.at[n, slot],
+                device_id=peer16(k),
+                device_id_type=MESH,
+            )
+
+        def spread(k, slot):
+            return pltpu.make_async_remote_copy(
+                src_ref=out.at[core, slot],
+                dst_ref=out.at[core, slot],
+                send_sem=a3_s.at[n, k],
+                recv_sem=a3_r.at[n, slot],
+                device_id=peer16(k),
+                device_id_type=MESH,
+            )
+
+        def last(slot):
+            return pltpu.make_async_remote_copy(
+                src_ref=out.at[core],
+                dst_ref=out.at[slot],
+                send_sem=a4_s.at[n],
+                recv_sem=a4_r.at[n],
+                device_id=sibling,
+                device_id_type=MESH,
+            )
+
+        start_y, wait_y = exchange(r2, 4, y, peer_y, a2_s.at[n], a2_r.at[n])
+
+        def step0():
+            swap().start()
+
+        def step1():
+            swap().wait()
+            r0[...] = r0[...] + gb[core]
+            for k in others:
+                scatter(k, place16).start()
+            r1[place16] = r0[place16]
+
+        def step2():
+            for k in others:
+                scatter(k, k).wait_recv()
+            r2[y] = jnp.sum(r1[...], axis=0)
+            start_y()
+
+        def step3():
+            wait_y()
+            out[core, place16] = jnp.sum(r2[...], axis=0)
+            for k in others:
+                spread(k, place16).start()
+
+        def step4():
+            for k in others:
+                spread(k, k).wait_recv()
+            last(core).start()
+
+        def step5():
+            for k in others:
+                scatter(k, place16).wait_send()
+                spread(k, place16).wait_send()
+            last(core).wait_send()
+            last(1 - core).wait_recv()
+
+        return step0, step1, step2, step3, step4, step5
+
+    first = all_reduce(0, gb0, r00, r10, r20, mlp_out)
+    second = all_reduce(1, gb1, r01, r11, r21, att_out)
+    for h in range(2):
+        gb0[h] = mlp[h].reshape(16, 16, WIDTH)
+    first[0]()
+
+    for ab in range(4):
+        rows = slice(ab * 32, ab * 32 + 32)
+
+        def add(i, carry):
+            p, e = carry
+            for j in range(OWN):
+                g = pre[i, j, rows, :]
+                p = p + g * cand_scale[pl.ds(i * OWN + j, 1), :]
+                e = e + g * row_scale[pl.ds(i * OWN + j, 1), :]
+            return p, e
+
+        zero = jnp.zeros((32, WIDTH), F32)
+        p, e = lax.fori_loop(0, USERS, add, (zero, zero))
+        gb1[0, ab * 4 : ab * 4 + 4] = p.reshape(4, 8, WIDTH)
+        gb1[1, ab * 4 : ab * 4 + 4] = e.reshape(4, 8, WIDTH)
+        if ab == 1:
+            first[1]()
+    second[0]()
+    lane = lax.broadcasted_iota(jnp.int32, (OWN_ALL, 128), 1)
+    sub = lax.broadcasted_iota(jnp.int32, (OWN_ALL, 128), 0)
+    scale_row = diag_row(row_scale[:, :128])
+    g_row = diag_row(jnp.sum(unit_sums[...] * scale_row, axis=1, keepdims=True))
     sm1[place8] = jnp.concatenate(
         [
             jnp.concatenate([g_row, jnp.zeros_like(g_row)], axis=1),
-            hidden_grad,
-            output_grad,
+            jnp.sum(dh[0], axis=0, keepdims=True),
+            jnp.sum(dh[1], axis=0, keepdims=True),
             jnp.zeros((5, WIDTH), F32),
         ],
         axis=0,
     )
-    small_start, small_wait = exchange(sm1, 8, place8, peer8, sm1_s, sm1_r)
-    small_start()
-
-    def put(first, value):
-        for c in range(value.shape[0] // 8):
-            at = first // 8 + c
-            half, rest = divmod(at, 48)
-            gb[half, rest // 3, (rest % 3) * 8 : (rest % 3) * 8 + 8, :] = value[c * 8 : c * 8 + 8, :]
-
-    put(0, pg[...])
-    put(128, eg[...])
-    put(256, mlp[0])
-    put(512, mlp[1])
-
-    swap = pltpu.make_async_remote_copy(
-        src_ref=gb.at[1 - core],
-        dst_ref=r0,
-        send_sem=a0_s,
-        recv_sem=a0_r,
-        device_id=sibling,
-        device_id_type=MESH,
-    )
-    swap.start()
-    small_wait()
+    start, wait = exchange(sm1, 8, place8, peer8, sm1_s, sm1_r)
+    start()
+    second[1]()
+    first[2]()
+    wait()
     sm2[place16] = jnp.sum(sm1[...], axis=0)
-    small_start, small_wait = exchange(sm2, 16, place16, peer16, sm2_s, sm2_r)
-    small_start()
-    swap.wait()
-    r0[...] = r0[...] + gb[core]
-
-    def scatter(k, slot):
-        return pltpu.make_async_remote_copy(
-            src_ref=r0.at[k],
-            dst_ref=r1.at[slot],
-            send_sem=a1_s.at[k],
-            recv_sem=a1_r.at[slot],
-            device_id=peer16(k),
-            device_id_type=MESH,
-        )
-
-    others = [(place16 + d) % 16 for d in range(1, 16)]
-    for k in others:
-        scatter(k, place16).start()
-    r1[place16] = r0[place16]
-    for k in others:
-        scatter(k, k).wait_recv()
-    r2[y] = jnp.sum(r1[...], axis=0)
-    start, wait = exchange(r2, 4, y, peer_y, a2_s, a2_r)
+    start, wait = exchange(sm2, 16, place16, peer16, sm2_s, sm2_r)
     start()
+    second[2]()
+    first[3]()
+    second[3]()
     wait()
-    grads_out[core, place16] = jnp.sum(r2[...], axis=0)
-
-    def spread(k, slot):
-        return pltpu.make_async_remote_copy(
-            src_ref=grads_out.at[core, slot],
-            dst_ref=grads_out.at[core, slot],
-            send_sem=a3_s.at[k],
-            recv_sem=a3_r.at[slot],
-            device_id=peer16(k),
-            device_id_type=MESH,
-        )
-
-    for k in others:
-        spread(k, place16).start()
-    for k in others:
-        scatter(k, place16).wait_send()
-    small_wait()
     small_out[...] = jnp.sum(sm2[...], axis=0)
-    for k in others:
-        spread(k, k).wait_recv()
-    last = pltpu.make_async_remote_copy(
-        src_ref=grads_out.at[core],
-        dst_ref=grads_out.at[core],
-        send_sem=a4_s,
-        recv_sem=a4_r,
-        device_id=sibling,
-        device_id_type=MESH,
-    )
-    last.start()
-    for k in others:
-        spread(k, place16).wait_send()
-    last.wait_send()
-    pltpu.make_async_remote_copy(
-        src_ref=grads_out.at[core],
-        dst_ref=grads_out.at[1 - core],
-        send_sem=a4_s,
-        recv_sem=a4_r,
-        device_id=sibling,
-        device_id_type=MESH,
-    ).wait_recv()
+    first[4]()
+    second[4]()
+    first[5]()
+    second[5]()
 
 
 def finish_kernel(
     logits,
-    grads,
+    mlp,
+    att,
     small,
     pair_weight,
     event_weight,
@@ -636,10 +727,11 @@
     hidden_out,
     output_out,
 ):
-    flat = grads[...].reshape(768, WIDTH)
+    flat = mlp[...].reshape(512, WIDTH)
+    attention = att[...].reshape(256, WIDTH)
     w = weigher[...]
-    pair = jnp.transpose(flat[:128])
-    event = jnp.transpose(flat[128:256])
+    pair = jnp.transpose(attention[:128])
+    event = jnp.transpose(attention[128:])
     g = small[0:1, :128]
     pair_out[...] = pair * w
     event_out[...] = event * w
@@ -647,8 +739,8 @@
     weigher_out[...] = scoring_bias[...] * g + jnp.sum(
         pair * pair_weight[...] + event * event_weight[...], axis=0, keepdims=True
     )
-    pooling_out[...] = flat[256:512]
-    itemwise_out[...] = flat[512:768]
+    pooling_out[...] = flat[:256]
+    itemwise_out[...] = flat[256:]
     hidden_out[...] = small[1:2, :]
     output_out[...] = small[2:3, :]
     logits_out[...] = logits[:, :OWN]
@@ -677,24 +769,36 @@
     vmem = pl.BlockSpec(memory_space=pltpu.VMEM)
     row = lambda v: v.reshape(1, -1)
     dma = pltpu.SemaphoreType.DMA
-    logits, grads, small = pl.pallas_call(
+    logits, mlp, att, small = pl.pallas_call(
         main_kernel,
         out_shape=(
             jax.ShapeDtypeStruct((USERS, 128), F32),
-            jax.ShapeDtypeStruct((2, 16, 24, WIDTH), F32),
+            jax.ShapeDtypeStruct((2, 16, 16, WIDTH), F32),
+            jax.ShapeDtypeStruct((2, 16, 8, WIDTH), F32),
             jax.ShapeDtypeStruct((8, WIDTH), F32),
         ),
         in_specs=[
             pl.BlockSpec(memory_space=pltpu.SMEM),
-            pl.BlockSpec(memory_space=pl.ANY),
         ]
-        + [vmem] * 16,
-        out_specs=(vmem, vmem, vmem),
+        + [pl.BlockSpec(memory_space=pl.ANY)] * 9
+        + [vmem] * 8,
+        out_specs=(vmem,) * 4,
         scratch_shapes=[
             pltpu.VMEM((USERS, EVENTS, WIDTH), BF16),
+            pltpu.VMEM((USERS, CAND_DEV, WIDTH), BF16),
+            pltpu.VMEM((USERS, SHORT, WIDTH), BF16),
+            pltpu.VMEM((WIDTH, WIDTH), BF16),
+            pltpu.VMEM((WIDTH, WIDTH), BF16),
+            pltpu.VMEM((WIDTH, SCORE_H), F32),
+            pltpu.VMEM((WIDTH, SCORE_H), F32),
+            pltpu.VMEM((WIDTH, WIDTH), F32),
+            pltpu.VMEM((WIDTH, WIDTH), F32),
             pltpu.VMEM((CAND_DEV, WIDTH), BF16),
             pltpu.VMEM((CAND_DEV, EVENTS), F32),
             pltpu.VMEM((CAND_DEV, EVENTS), BF16),
+            pltpu.VMEM((CAND_DEV, 128), F32),
+            pltpu.VMEM((CAND_DEV, 128), F32),
+            pltpu.VMEM((CAND_DEV, 128), F32),
             pltpu.VMEM((CAND_DEV, 128), F32),
             pltpu.VMEM((CAND_DEV, 128), F32),
             pltpu.VMEM((USERS, BLOCKS, OWN, WIDTH), F32),
@@ -710,27 +814,33 @@
             pltpu.VMEM((SCORE_H, WIDTH), F32),
             pltpu.VMEM((SCORE_H, WIDTH), F32),
             pltpu.VMEM((SCORE_H, WIDTH), F32),
-            pltpu.VMEM((2, CGROUP * SCORE_H, WIDTH), BF16),
+            pltpu.VMEM((OWN // CGROUP, 2, CGROUP * SCORE_H, WIDTH), BF16),
             pltpu.VMEM((USERS, OWN, SCORE_H, SHORT), F32),
             pltpu.VMEM((USERS, OWN, SHORT), F32),
             pltpu.VMEM((USERS, OWN, WIDTH), F32),
             pltpu.VMEM((USERS, OWN, SHORT), F32),
-            pltpu.VMEM((SCORE_H, WIDTH), F32),
-            pltpu.VMEM((SCORE_H, SHORT), F32),
-            pltpu.VMEM((SCORE_H, SHORT), F32),
-            pltpu.VMEM((SCORE_H, WIDTH), F32),
+            pltpu.VMEM((2, OWN_ALL, 128), F32),
+            pltpu.VMEM((SCORE_H, OWN_ALL), F32),
+            pltpu.VMEM((OWN_ALL, WIDTH), F32),
+            pltpu.VMEM((OWN_ALL, WIDTH), F32),
             pltpu.VMEM((2, WIDTH, OWN_ALL), F32),
-            pltpu.VMEM((OWN_ALL, WIDTH), F32),
+            pltpu.VMEM((2, OWN_ALL, WIDTH), F32),
             pltpu.VMEM((2, WIDTH, WIDTH), F32),
             pltpu.VMEM((8, 2, USERS, 128), F32),
             pltpu.VMEM((16, 2, USERS, 128), F32),
             pltpu.VMEM((8, 8, WIDTH), F32),
             pltpu.VMEM((16, 8, WIDTH), F32),
-            pltpu.VMEM((2, 16, 24, WIDTH), F32),
-            pltpu.VMEM((16, 24, WIDTH), F32),
-            pltpu.VMEM((16, 24, WIDTH), F32),
-            pltpu.VMEM((4, 24, WIDTH), F32),
+            pltpu.VMEM((2, 16, 16, WIDTH), F32),
+            pltpu.VMEM((2, 16, 8, WIDTH), F32),
+            pltpu.VMEM((16, 16, WIDTH), F32),
+            pltpu.VMEM((16, 8, WIDTH), F32),
+            pltpu.VMEM((16, 16, WIDTH), F32),
+            pltpu.VMEM((16, 8, WIDTH), F32),
+            pltpu.VMEM((4, 16, WIDTH), F32),
+            pltpu.VMEM((4, 8, WIDTH), F32),
             dma((USERS,)),
+            dma((USERS,)),
+            dma((7,)),
             dma((5, USERS)),
             dma((5, USERS)),
             dma((5, USERS)),
@@ -743,16 +853,16 @@
             dma((8,)),
             dma((16,)),
             dma((16,)),
-            dma,
-            dma,
-            dma((16,)),
-            dma((16,)),
-            dma((4,)),
-            dma((4,)),
-            dma((16,)),
-            dma((16,)),
-            dma,
-            dma,
+            dma((2,)),
+            dma((2,)),
+            dma((2, 16)),
+            dma((2, 16)),
+            dma((2, 4)),
+            dma((2, 4)),
+            dma((2, 16)),
+            dma((2, 16)),
+            dma((2,)),
+            dma((2,)),
         ],
         compiler_params=pltpu.CompilerParams(
             collective_id=0, has_side_effects=True, vmem_limit_bytes=62 * 1024 * 1024
@@ -763,18 +873,18 @@
         history,
         candidates,
         short_hist,
+        value_weight,
+        head_weight,
+        pair_weight,
+        event_weight,
+        pooling_weight,
+        itemwise_weight,
         pad_mask,
         short_mask,
         row(query_gain),
-        value_weight,
-        head_weight,
         row(head_vector),
-        pair_weight,
-        event_weight,
         row(scoring_bias),
         row(weigher),
-        pooling_weight,
-        itemwise_weight,
         row(hidden_bias),
         row(output_vector),
     )
@@ -791,10 +901,10 @@
             jax.ShapeDtypeStruct((1, WIDTH), F32),
             jax.ShapeDtypeStruct((1, WIDTH), F32),
         ),
-        in_specs=[vmem] * 7,
+        in_specs=[vmem] * 8,
         out_specs=(vmem,) * 9,
         name="finish_kernel",
-    )(logits, grads, small, pair_weight, event_weight, row(scoring_bias), row(weigher))
+    )(logits, mlp, att, small, pair_weight, event_weight, row(scoring_bias), row(weigher))
     flat = lambda v: v.reshape(-1)
     return (
         out[0],

time: 139 us -> 97.2 us (0.70)
  Pallas kernels: 138 us -> 96.4 us
    pallas_call x1, Pallas kernels: 136 us -> 94.2 us  [body(): pl.pallas_call(main_kernel, out_shape=(jax.ShapeDtypeStruct((USERS, 128),...]
where the time goes in v2:
time: 97.2 us; the launch traced here: 97 us
  Pallas kernels  96.4 us (99%)
    pallas_call x1, Pallas kernels, body(): pl.pallas_call(main_kernel, out_shape=(jax.ShapeDtypeStruct((USERS, 128),...  94.2 us
    pallas_call x1, Pallas kernels, body(): pl.pallas_call(finish_kernel, out_shape=(jax.ShapeDtypeStruct((USERS, OWN...  2.16 us

profile of v2, /device:TPU:1, one launch (start us, length us, event | category | flops | bytes accessed | tf_op | source)
XLA Modules:
  0.0 97.0 jit_solution(6638139372797346138)
XLA Ops:
  0.6 94.2 %main_kernel.1 = (f32[8,128]{1,0:T(8,128)}, f32[2,16,16,256]{3,2,1,0:T(8,128)}, f32[2,16,8,256]{3,2,1,0:T(8,128)}, f32[8,256]{1,0:T(8,128)}) custom-call(s32[8]{0:T(128)} %lengths.1, bf16[8,2048,256]{2,1,0:T(8,128)(2,1)} %history.1, bf16[8,512,256]{2,1,0:T(8,128)(2,1)} %candidates_hbm.1, bf16[8,256,256]{2,1,0:T(8,128)(2,1)} %short_hbm.1, ...), custom_call_target="tpu_custom_call" | custom-call | tf_op jit(solution)/shard_map/main_kernel/pallas_call | solution.py:772
  94.9 2.2 %finish_kernel.1 = (f32[8,16]{1,0:T(8,128)}, f32[256,128]{1,0:T(8,128)}, f32[256,128]{1,0:T(8,128)}, f32[1,128]{1,0:T(1,128)}, f32[1,128]{1,0:T(1,128)}, /*index...) custom-call(f32[8,128]{1,0:T(8,128)} %get-tuple-element.22.logits, ...), custom_call_target="tpu_custom_call" | custom-call | tf_op jit(solution)/shard_map/finish_kernel/pallas_call | solution.py:891

commit v3 on v2

--- a/solution.py
+++ b/solution.py
@@ -11,7 +11,6 @@
 NEG_FILL = -1e30
 NEG_CLAMP = -1e29
 SOFT_CAP = 10.0
-HIGHEST = lax.Precision.HIGHEST
 F32 = jnp.float32
 BF16 = jnp.bfloat16
 MESH = pl.DeviceIdType.MESH
@@ -26,8 +25,8 @@
 BLOCKS = 32
 OWN_ALL = USERS * OWN
 CGROUP = 4
-DELAY = (3, 5, 7, 9, 11)
-SLOTS = USERS + DELAY[4]
+DELAY = (5, 8, 10)
+SLOTS = max(USERS + DELAY[2], 2 * USERS)
 GELU_K = math.sqrt(2.0 / math.pi)
 GELU_C = 0.044715
 
@@ -36,6 +35,25 @@
     return lax.dot_general(
         a, b, (((ca,), (cb,)), ((), ())), precision=precision, preferred_element_type=F32
     )
+
+
+def halves(a):
+    high = a.astype(BF16)
+    return high, (a - high.astype(F32)).astype(BF16)
+
+
+def dot_split(a, b, cb=0):
+    n = a.shape[0]
+    both = dot(jnp.concatenate(halves(a), axis=0), b, 1, cb)
+    return both[:n] + both[n:]
+
+
+def dot_split2(a, b, cb=0):
+    n = a.shape[0]
+    a_high, a_low = halves(a)
+    b_high, b_low = halves(b)
+    both = dot(jnp.concatenate([a_high, a_low], axis=0), b_high, 1, cb)
+    return both[:n] + both[n:] + dot(a_high, b_low, 1, cb)
 
 
 def gelu(p):
@@ -63,6 +81,18 @@
     event_hbm,
     pooling_hbm,
     itemwise_hbm,
+    pad_hbm,
+    mask_hbm,
+    gain_hbm,
+    vector_hbm,
+    scoring_hbm,
+    weigher_hbm,
+    bias_hbm,
+    output_hbm,
+    logits_hbm,
+    mlp_hbm,
+    att_hbm,
+    small_hbm,
     pad_mask,
     short_mask,
     query_gain,
@@ -97,8 +127,6 @@
     rv0,
     rv1,
     rv2,
-    rv3,
-    rv4,
     rl,
     oc,
     pw_t,
@@ -109,6 +137,7 @@
     pre,
     att,
     interest,
+    dint,
     datt,
     exps,
     unit_sums,
@@ -132,6 +161,8 @@
     hist_sem,
     cand_sem,
     load_sem,
+    early_sem,
+    result_sem,
     rs_vs,
     rs_vr,
     rs_ls,
@@ -163,8 +194,20 @@
         (itemwise_hbm, itemwise_weight),
         (value_hbm, value_weight),
         (head_hbm, head_weight),
-    )
-    rv = (rv0, rv1, rv2, rv3, rv4)
+        (mask_hbm, short_mask),
+        (vector_hbm, head_vector),
+        (scoring_hbm, scoring_bias),
+        (weigher_hbm, weigher),
+        (bias_hbm, hidden_bias),
+        (output_hbm, output_vector),
+    )
+    results = (
+        (logits_out, logits_hbm),
+        (mlp_out, mlp_hbm),
+        (att_out, att_hbm),
+        (small_out, small_hbm),
+    )
+    rv = (rv0, rv1, rv2)
     cand = lax.axis_index("cand")
     ctx = lax.axis_index("ctx")
     x = ctx % 4
@@ -193,9 +236,21 @@
     def cand_copy(u):
         return pltpu.make_async_copy(candidates_hbm.at[u], candidates.at[u], cand_sem.at[u])
 
+    def early(k):
+        src, dst = ((pad_hbm, pad_mask), (gain_hbm, query_gain))[k]
+        return pltpu.make_async_copy(src, dst, early_sem.at[k])
+
+    def result(k):
+        return pltpu.make_async_copy(results[k][0], results[k][1], result_sem.at[k])
+
     def load(k):
         return pltpu.make_async_copy(loads[k][0], loads[k][1], load_sem.at[k])
 
+    for k in range(2):
+        early(k).start()
+    for u in range(2):
+        cand_copy(u).start()
+        hist_copy(u).start()
     barrier = pltpu.get_barrier_semaphore()
     for d in range(1, 8):
         pl.semaphore_signal(barrier, inc=1, device_id=peer8((place8 + d) % 8), device_id_type=MESH)
@@ -203,11 +258,8 @@
         pl.semaphore_signal(
             barrier, inc=1, device_id=peer16((place16 + d) % 16), device_id_type=MESH
         )
-    for u in range(USERS):
-        cand_copy(u).start()
-        hist_copy(u).start()
-    for k in range(len(loads)):
-        load(k).start()
+    for k in range(2):
+        early(k).wait()
 
     def set_up():
         for k in range(len(loads)):
@@ -228,101 +280,68 @@
     stride2 = 8 - 7 * core
     c1 = (ctx // stride1) % 4
     c2 = (ctx // stride2) % 4
-
-    def bits_of(c):
-        low, high = c % 2, c // 2
-        return low + high - 2 * low * high, high
-
-    def rs_plan(k, u):
-        q = u % 2
-        a1, b1 = bits_of(c1)
-        a2, b2 = bits_of(c2)
-        bits = (a1 + q * (b1 - a1), b1 + q * (a1 - b1), a2 + q * (b2 - a2), b2 + q * (a2 - b2), y_hi)
-        start = 0
-        for j in range(k):
-            start = start + bits[j] * (16 >> j)
-        n = 16 >> k
-        keep = start + bits[k] * n
-        send = start + (1 - bits[k]) * n
-        if k == 4:
-            partner = ctx + (1 - 2 * y_hi) * 4
-        else:
-            c, stride = (c1, stride1) if k < 2 else (c2, stride2)
-            pa = c + 1 - 2 * (c % 2)
-            pb = 3 - c
-            pc = pa + q * (pb - pa) if k % 2 == 0 else pb + q * (pa - pb)
-            partner = ctx + (pc - c) * stride
-        return (cand, partner), keep, send
-
-    def rs_copies(k, u):
-        device, _, send = rs_plan(k, u)
-        n = 16 >> k
+    stages = (
+        (c1, stride1, 4, 8, 0),
+        (c2, stride2, 4, 2, c1 * 8),
+        (y_hi, 4, 2, 1, c1 * 8 + c2 * 2),
+    )
+
+    def rs_copies(k, u, d):
+        c, stride, n, chunk, first = stages[k]
+        to = (c + d) % n
+        device = (cand, ctx + (to - c) * stride)
         value = pltpu.make_async_remote_copy(
-            src_ref=acc.at[u, pl.ds(send, n)],
-            dst_ref=rv[k].at[u],
-            send_sem=rs_vs.at[k, u],
-            recv_sem=rs_vr.at[k, u],
+            src_ref=acc.at[u, pl.ds(first + to * chunk, chunk)],
+            dst_ref=rv[k].at[u, d - 1],
+            send_sem=rs_vs.at[k, u, d - 1],
+            recv_sem=rs_vr.at[k, u, d - 1],
             device_id=device,
             device_id_type=MESH,
         )
-        if k == 0:
-            src, dst = lse.at[k, u, pl.ds(send // 8, 2)], rl.at[u, pl.ds(0, 2)]
-        else:
-            src, dst = lse.at[k, u, pl.ds(send // 8, 1)], rl.at[u, pl.ds(1 + k, 1)]
         weight = pltpu.make_async_remote_copy(
-            src_ref=src,
-            dst_ref=dst,
-            send_sem=rs_ls.at[k, u],
-            recv_sem=rs_lr.at[k, u],
+            src_ref=lse.at[k, u, to if k == 0 else c1],
+            dst_ref=rl.at[u, 3 * k + d - 1],
+            send_sem=rs_ls.at[k, u, d - 1],
+            recv_sem=rs_lr.at[k, u, d - 1],
             device_id=device,
             device_id_type=MESH,
         )
         return value, weight
 
     def rs_send(k, u):
-        for copy in rs_copies(k, u):
-            copy.start()
+        for d in (2, 1, 3) if k < 2 else (1,):
+            for copy in rs_copies(k, u, d):
+                copy.start()
 
     def rs_merge(k, u):
-        for copy in rs_copies(k, u):
-            copy.wait()
-        _, keep, _ = rs_plan(k, u)
-        n = 16 >> k
-        rows = 2 if k == 0 else 1
-        per_row = min(n, 8)
-        for r in range(rows):
-            row = keep // 8 + r
-            mine = lse[k, u, row]
-            other = rl[u, (r if k == 0 else 1 + k)]
-            top = jnp.maximum(mine, other)
-            e_mine = jnp.exp(mine - top)
-            e_other = jnp.exp(other - top)
-            total = e_mine + e_other
-            share = e_other / total
-            if k < 4:
-                lse[k + 1, u, row] = top + jnp.log(total)
-            share16 = jnp.concatenate([share, share], axis=0)
-            lane = lax.broadcasted_iota(jnp.int32, (16, 128), 1)
-            sub = lax.broadcasted_iota(jnp.int32, (16, 128), 0)
-            for b in range(per_row):
-                at = keep + r * 8 + b
-                off = (at % 8) * 16
-                col = jnp.sum(
-                    jnp.where(lane - sub == off, share16, 0.0), axis=1, keepdims=True
-                )
-                own = acc[u, at]
-                got = rv[k][u, r * 8 + b]
-                acc[u, at] = own + col * (got - own)
+        c, stride, n, chunk, first = stages[k]
+        for d in range(1, n):
+            for copy in rs_copies(k, u, d):
+                copy.wait()
+        logs = [lse[k, u, c1]] + [rl[u, 3 * k + d - 1] for d in range(1, n)]
+        top = functools.reduce(jnp.maximum, logs)
+        parts = [jnp.exp(v - top) for v in logs]
+        total = functools.reduce(jnp.add, parts)
+        if k < 2:
+            lse[k + 1, u, c1] = top + jnp.log(total)
+        shares = [jnp.concatenate([p / total] * 2, axis=0) for p in parts]
+        lane = lax.broadcasted_iota(jnp.int32, (16, 128), 1)
+        sub = lax.broadcasted_iota(jnp.int32, (16, 128), 0)
+        for b in range(chunk):
+            at = first + c * chunk + b
+            here = lane - sub == (at % 8) * 16
+            sum_ = None
+            for j, share in enumerate(shares):
+                col = jnp.sum(jnp.where(here, share, 0.0), axis=1, keepdims=True)
+                term = col * (acc[u, at] if j == 0 else rv[k][u, j - 1, b])
+                sum_ = term if sum_ is None else sum_ + term
+            acc[u, at] = sum_
 
     def teacher_user(u):
-        q = u % 2
         gain = query_gain[...] * (1.0 / 16.0)
         cand_copy(u).wait()
         for pos in range(BLOCKS):
-            p4, p3, p2, p1, p0 = ((pos >> s) & 1 for s in (4, 3, 2, 1, 0))
-            first = 2 * (p3 + q * (p4 - p3)) + (p4 ^ p3)
-            second = 2 * (p1 + q * (p2 - p1)) + (p2 ^ p1)
-            block = first * stride1 + second * stride2 + p0 * 4
+            block = (pos // 8) * stride1 + (pos // 2 % 4) * stride2 + (pos % 2) * 4
             rows = candidates[u, pl.ds(pl.multiple_of(block * 16, 16), 16), :]
             qs[pos * 16 : pos * 16 + 16, :] = (rows.astype(F32) * gain).astype(BF16)
         spot = lax.broadcasted_iota(jnp.int32, (1, EVENTS), 1) + ctx * EVENTS
@@ -388,14 +407,15 @@
                     jnp.maximum(pj, 0.0) * w_full[...], axis=0, keepdims=True
                 )
         weights = jnp.where(short_ok(u), att[u], 0.0)
-        interest[u] = dot(weights, short[u].astype(F32), 1, 0, HIGHEST)
+        interest[u] = dot_split(weights, short[u])
 
     def back_user(u):
+        datt[...] = jnp.where(short_ok(u), dot_split(dint[u], short[u], 1), 0.0)
         for cg in range(OWN // CGROUP):
             cols = []
             for j in range(CGROUP):
                 c = cg * CGROUP + j
-                m = jnp.where(pre[u, c] > 0.0, datt[u, pl.ds(c, 1), :], 0.0)
+                m = jnp.where(pre[u, c] > 0.0, datt[c : c + 1, :], 0.0)
                 wb[cg, 0, j * 128 : j * 128 + 128, :] = m.astype(BF16)
                 cols.append(jnp.sum(m, axis=1, keepdims=True))
             g = dot(wb[cg, 0], short[u])
@@ -408,17 +428,27 @@
             unit_sums[...] = units
 
     def reduce_steps(i):
-        for k in reversed(range(5)):
+        for k in reversed(range(3)):
             u = i - DELAY[k]
 
             def step(k=k, u=u):
                 rs_merge(k, u)
-                if k < 4:
+                if k < 2:
                     rs_send(k + 1, u)
 
             pl.when((u >= 0) & (u < USERS))(step)
 
     def teacher_slot(i, carry):
+        @pl.when(i + 2 < USERS)
+        def _():
+            cand_copy(i + 2).start()
+            hist_copy(i + 2).start()
+
+        @pl.when(i == USERS - 2)
+        def _():
+            for k in range(len(loads)):
+                load(k).start()
+
         teacher_user(i)
 
         @pl.when(i == 0)
@@ -442,8 +472,8 @@
     own_all = oc[...].reshape(OWN_ALL, WIDTH)
     inter = interest[...].reshape(OWN_ALL, WIDTH)
     hid = (
-        dot(inter, pooling_weight[...], 1, 0, HIGHEST)
-        + dot(own_all, itemwise_weight[...], 1, 0, HIGHEST)
+        dot_split2(inter, pooling_weight[...])
+        + dot_split2(own_all, itemwise_weight[...])
         + hidden_bias[...]
     )
     th = jnp.tanh(GELU_K * (hid + GELU_C * hid * hid * hid))
@@ -454,10 +484,8 @@
     s_tanh = jnp.tanh(jnp.sum(s_hidden * output_vector[...], axis=1, keepdims=True) / SOFT_CAP)
     draw = 1.0 - s_tanh * s_tanh
     dhid = draw * output_vector[...] * slope
-    dinter = dot(dhid, pooling_weight[...], 1, 1, HIGHEST)
-    for u in range(USERS):
-        d = dot(dinter[u * OWN : u * OWN + OWN, :], short[u].astype(F32), 1, 1, HIGHEST)
-        datt[u] = jnp.where(short_ok(u), d, 0.0)
+    dinter = dot_split2(dhid, pooling_weight[...], 1)
+    dint[...] = dinter.reshape(USERS, OWN, WIDTH)
     dh[0] = dhid
     dh[1] = s_hidden * draw
     s_exp = jnp.broadcast_to(jnp.exp(SOFT_CAP * s_tanh), (OWN_ALL, 128))
@@ -475,9 +503,8 @@
     own_all = oc[...].reshape(OWN_ALL, WIDTH)
     parts = []
     for u in range(USERS):
-        _, keep, _ = rs_plan(4, u)
-        parts.append(acc[u, keep])
-    pooled = dot(jnp.concatenate(parts, axis=0), value_weight[...].astype(F32), 1, 0, HIGHEST)
+        parts.append(acc[u, c1 * 8 + c2 * 2 + y_hi])
+    pooled = dot_split(jnp.concatenate(parts, axis=0), value_weight[...])
     normed = pooled * lax.rsqrt(jnp.mean(pooled * pooled, axis=1, keepdims=True) + 1e-6)
     mixed = (normed * own_all).astype(BF16)
     t_hidden = gelu(dot(mixed, head_weight[...]))
@@ -492,6 +519,8 @@
         ),
         axis=1,
     )
+
+    result(0).start()
 
     t_exp = jnp.broadcast_to(jnp.exp(t_logit), (OWN_ALL, 128))
     exps[1] = t_exp
@@ -545,12 +574,12 @@
     done = SLOTS - 2 * USERS
     start, wait = exchange(st1, 8, place8, peer8, st1_s, st1_r)
     start()
-    more_back(done, done + 3)
+    more_back(done, (done + USERS) // 2)
     wait()
     st2[place16] = jnp.sum(st1[...], axis=0)
     start, wait = exchange(st2, 16, place16, peer16, st2_s, st2_r)
     start()
-    more_back(done + 3, USERS)
+    more_back((done + USERS) // 2, USERS)
     wait()
     sums = jnp.sum(st2[...], axis=0)
 
@@ -566,7 +595,7 @@
     dh[1] = dh[1] * row_scale[...]
 
     def mlp_half(h, carry):
-        mlp[h] = dot(rows_t[h], dh[0], 1, 0, HIGHEST)
+        mlp[h] = dot_split2(rows_t[h], dh[0])
         return carry
 
     lax.fori_loop(0, 2, mlp_half, 0)
@@ -658,8 +687,8 @@
         gb0[h] = mlp[h].reshape(16, 16, WIDTH)
     first[0]()
 
-    for ab in range(4):
-        rows = slice(ab * 32, ab * 32 + 32)
+    for ab in range(2):
+        rows = slice(ab * 64, ab * 64 + 64)
 
         def add(i, carry):
             p, e = carry
@@ -669,11 +698,11 @@
                 e = e + g * row_scale[pl.ds(i * OWN + j, 1), :]
             return p, e
 
-        zero = jnp.zeros((32, WIDTH), F32)
+        zero = jnp.zeros((64, WIDTH), F32)
         p, e = lax.fori_loop(0, USERS, add, (zero, zero))
-        gb1[0, ab * 4 : ab * 4 + 4] = p.reshape(4, 8, WIDTH)
-        gb1[1, ab * 4 : ab * 4 + 4] = e.reshape(4, 8, WIDTH)
-        if ab == 1:
+        gb1[0, ab * 8 : ab * 8 + 8] = p.reshape(8, 8, WIDTH)
+        gb1[1, ab * 8 : ab * 8 + 8] = e.reshape(8, 8, WIDTH)
+        if ab == 0:
             first[1]()
     second[0]()
     lane = lax.broadcasted_iota(jnp.int32, (OWN_ALL, 128), 1)
@@ -702,10 +731,15 @@
     second[3]()
     wait()
     small_out[...] = jnp.sum(sm2[...], axis=0)
+    result(3).start()
     first[4]()
     second[4]()
     first[5]()
+    result(1).start()
     second[5]()
+    result(2).start()
+    for k in range(4):
+        result(k).wait()
 
 
 def finish_kernel(
@@ -780,10 +814,21 @@
         in_specs=[
             pl.BlockSpec(memory_space=pltpu.SMEM),
         ]
-        + [pl.BlockSpec(memory_space=pl.ANY)] * 9
-        + [vmem] * 8,
-        out_specs=(vmem,) * 4,
+        + [pl.BlockSpec(memory_space=pl.ANY)] * 17,
+        out_specs=(pl.BlockSpec(memory_space=pl.ANY),) * 4,
         scratch_shapes=[
+            pltpu.VMEM((USERS, EVENTS), jnp.int32),
+            pltpu.VMEM((USERS, SHORT), jnp.int32),
+            pltpu.VMEM((1, WIDTH), F32),
+            pltpu.VMEM((1, WIDTH), F32),
+            pltpu.VMEM((1, SCORE_H), F32),
+            pltpu.VMEM((1, SCORE_H), F32),
+            pltpu.VMEM((1, WIDTH), F32),
+            pltpu.VMEM((1, WIDTH), F32),
+            pltpu.VMEM((USERS, 128), F32),
+            pltpu.VMEM((2, 16, 16, WIDTH), F32),
+            pltpu.VMEM((2, 16, 8, WIDTH), F32),
+            pltpu.VMEM((8, WIDTH), F32),
             pltpu.VMEM((USERS, EVENTS, WIDTH), BF16),
             pltpu.VMEM((USERS, CAND_DEV, WIDTH), BF16),
             pltpu.VMEM((USERS, SHORT, WIDTH), BF16),
@@ -802,13 +847,11 @@
             pltpu.VMEM((CAND_DEV, 128), F32),
             pltpu.VMEM((CAND_DEV, 128), F32),
             pltpu.VMEM((USERS, BLOCKS, OWN, WIDTH), F32),
-            pltpu.VMEM((5, USERS, 4, 8, 128), F32),
-            pltpu.VMEM((USERS, 16, OWN, WIDTH), F32),
-            pltpu.VMEM((USERS, 8, OWN, WIDTH), F32),
-            pltpu.VMEM((USERS, 4, OWN, WIDTH), F32),
-            pltpu.VMEM((USERS, 2, OWN, WIDTH), F32),
-            pltpu.VMEM((USERS, 1, OWN, WIDTH), F32),
-            pltpu.VMEM((USERS, 6, 8, 128), F32),
+            pltpu.VMEM((3, USERS, 4, 8, 128), F32),
+            pltpu.VMEM((USERS, 3, 8, OWN, WIDTH), F32),
+            pltpu.VMEM((USERS, 3, 2, OWN, WIDTH), F32),
+            pltpu.VMEM((USERS, 1, 1, OWN, WIDTH), F32),
+            pltpu.VMEM((USERS, 7, 8, 128), F32),
             pltpu.VMEM((USERS, OWN, WIDTH), F32),
             pltpu.VMEM((SCORE_H, WIDTH), F32),
             pltpu.VMEM((SCORE_H, WIDTH), F32),
@@ -818,7 +861,8 @@
             pltpu.VMEM((USERS, OWN, SCORE_H, SHORT), F32),
             pltpu.VMEM((USERS, OWN, SHORT), F32),
             pltpu.VMEM((USERS, OWN, WIDTH), F32),
-            pltpu.VMEM((USERS, OWN, SHORT), F32),
+            pltpu.VMEM((USERS, OWN, WIDTH), F32),
+            pltpu.VMEM((OWN, SHORT), F32),
             pltpu.VMEM((2, OWN_ALL, 128), F32),
             pltpu.VMEM((SCORE_H, OWN_ALL), F32),
             pltpu.VMEM((OWN_ALL, WIDTH), F32),
@@ -840,11 +884,13 @@
             pltpu.VMEM((4, 8, WIDTH), F32),
             dma((USERS,)),
             dma((USERS,)),
-            dma((7,)),
-            dma((5, USERS)),
-            dma((5, USERS)),
-            dma((5, USERS)),
-            dma((5, USERS)),
+            dma((13,)),
+            dma((2,)),
+            dma((4,)),
+            dma((3, USERS, 3)),
+            dma((3, USERS, 3)),
+            dma((3, USERS, 3)),
+            dma((3, USERS, 3)),
             dma((8,)),
             dma((8,)),
             dma((16,)),

time: 97.2 us -> 88.9 us (0.915)
  Pallas kernels: 96.4 us -> 88.1 us
    pallas_call x1, Pallas kernels: 94.2 us -> 85.9 us  [body(): pl.pallas_call(main_kernel, out_shape=(jax.ShapeDtypeStruct((USERS, 128),...]
where the time goes in v3:
time: 88.9 us; the launch traced here: 88.7 us
  Pallas kernels  88.1 us (99%)
    pallas_call x1, Pallas kernels, body(): pl.pallas_call(main_kernel, out_shape=(jax.ShapeDtypeStruct((USERS, 128),...  85.9 us
    pallas_call x1, Pallas kernels, body(): pl.pallas_call(finish_kernel, out_shape=(jax.ShapeDtypeStruct((USERS, OWN...  2.16 us

profile of v3, /device:TPU:1, one launch (start us, length us, event | category | flops | bytes accessed | tf_op | source)
XLA Modules:
  0.0 88.7 jit_solution(7879765546659204668)
XLA Ops:
  0.6 85.9 %main_kernel.1 = (f32[8,128]{1,0:T(8,128)}, f32[2,16,16,256]{3,2,1,0:T(8,128)}, f32[2,16,8,256]{3,2,1,0:T(8,128)}, f32[8,256]{1,0:T(8,128)}) custom-call(s32[8]{0:T(128)} %lengths.1, bf16[8,2048,256]{2,1,0:T(8,128)(2,1)} %history.1, bf16[8,512,256]{2,1,0:T(8,128)(2,1)} %candidates_hbm.1, bf16[8,256,256]{2,1,0:T(8,128)(2,1)} %short_hbm.1, ...), custom_call_target="tpu_custom_call" | custom-call | tf_op jit(solution)/shard_map/main_kernel/pallas_call | solution.py:806
  86.6 2.2 %finish_kernel.1 = (f32[8,16]{1,0:T(8,128)}, f32[256,128]{1,0:T(8,128)}, f32[256,128]{1,0:T(8,128)}, f32[1,128]{1,0:T(1,128)}, f32[1,128]{1,0:T(1,128)}, /*index...) custom-call(f32[8,128]{1,0:T(8,128)} %get-tuple-element.22.logits, ...), custom_call_target="tpu_custom_call" | custom-call | tf_op jit(solution)/shard_map/finish_kernel/pallas_call | solution.py:937

commit v4 on v3

--- a/solution.py
+++ b/solution.py
@@ -760,24 +760,51 @@
     itemwise_out,
     hidden_out,
     output_out,
+    logits_v,
+    pair_v,
+    event_v,
+    scoring_v,
+    weigher_v,
+    hidden_v,
+    output_v,
+    out_sem,
 ):
-    flat = mlp[...].reshape(512, WIDTH)
-    attention = att[...].reshape(256, WIDTH)
+    outputs = (
+        (mlp.at[0], pooling_out),
+        (mlp.at[1], itemwise_out),
+        (pair_v, pair_out),
+        (event_v, event_out),
+        (scoring_v, scoring_out),
+        (weigher_v, weigher_out),
+        (hidden_v, hidden_out),
+        (output_v, output_out),
+        (logits_v, logits_out),
+    )
+
+    def give(k):
+        return pltpu.make_async_copy(outputs[k][0], outputs[k][1], out_sem.at[k])
+
+    for k in range(2):
+        give(k).start()
     w = weigher[...]
-    pair = jnp.transpose(attention[:128])
-    event = jnp.transpose(attention[128:])
+    pair = jnp.transpose(att[:128])
+    event = jnp.transpose(att[128:])
+    pair_v[...] = pair * w
+    event_v[...] = event * w
+    give(2).start()
+    give(3).start()
     g = small[0:1, :128]
-    pair_out[...] = pair * w
-    event_out[...] = event * w
-    scoring_out[...] = g * w
-    weigher_out[...] = scoring_bias[...] * g + jnp.sum(
+    scoring_v[...] = g * w
+    weigher_v[...] = scoring_bias[...] * g + jnp.sum(
         pair * pair_weight[...] + event * event_weight[...], axis=0, keepdims=True
     )
-    pooling_out[...] = flat[:256]
-    itemwise_out[...] = flat[256:]
-    hidden_out[...] = small[1:2, :]
-    output_out[...] = small[2:3, :]
-    logits_out[...] = logits[:, :OWN]
+    hidden_v[...] = small[1:2, :]
+    output_v[...] = small[2:3, :]
+    logits_v[...] = logits[:, :OWN]
+    for k in range(4, 9):
+        give(k).start()
+    for k in range(9):
+        give(k).wait()
 
 
 def body(
@@ -948,9 +975,19 @@
             jax.ShapeDtypeStruct((1, WIDTH), F32),
         ),
         in_specs=[vmem] * 8,
-        out_specs=(vmem,) * 9,
+        out_specs=(pl.BlockSpec(memory_space=pl.ANY),) * 9,
+        scratch_shapes=[
+            pltpu.VMEM((USERS, OWN), F32),
+            pltpu.VMEM((WIDTH, SCORE_H), F32),
+            pltpu.VMEM((WIDTH, SCORE_H), F32),
+            pltpu.VMEM((1, SCORE_H), F32),
+            pltpu.VMEM((1, SCORE_H), F32),
+            pltpu.VMEM((1, WIDTH), F32),
+            pltpu.VMEM((1, WIDTH), F32),
+            dma((9,)),
+        ],
         name="finish_kernel",
-    )(logits, mlp, att, small, pair_weight, event_weight, row(scoring_bias), row(weigher))
+    )(logits, mlp.reshape(2, WIDTH, WIDTH), att.reshape(256, WIDTH), small, pair_weight, event_weight, row(scoring_bias), row(weigher))
     flat = lambda v: v.reshape(-1)
     return (
         out[0],

time: 88.9 us -> 88.9 us (level)
  no operation moved by 1% of the time
where the time goes in v4:
time: 88.9 us; the launch traced here: 88.7 us
  Pallas kernels  88.1 us (99%)
    pallas_call x1, Pallas kernels, body(): pl.pallas_call(main_kernel, out_shape=(jax.ShapeDtypeStruct((USERS, 128),...  85.9 us
    pallas_call x1, Pallas kernels, body(): pl.pallas_call(finish_kernel, out_shape=(jax.ShapeDtypeStruct((USERS, OWN...  2.17 us

profile of v4, /device:TPU:1, one launch (start us, length us, event | category | flops | bytes accessed | tf_op | source)
XLA Modules:
  0.0 88.7 jit_solution(18164711594950995298)
XLA Ops:
  0.6 85.9 %main_kernel.1 = (f32[8,128]{1,0:T(8,128)}, f32[2,16,16,256]{3,2,1,0:T(8,128)}, f32[2,16,8,256]{3,2,1,0:T(8,128)}, f32[8,256]{1,0:T(8,128)}) custom-call(s32[8]{0:T(128)} %lengths.1, bf16[8,2048,256]{2,1,0:T(8,128)(2,1)} %history.1, bf16[8,512,256]{2,1,0:T(8,128)(2,1)} %candidates_hbm.1, bf16[8,256,256]{2,1,0:T(8,128)(2,1)} %short_hbm.1, ...), custom_call_target="tpu_custom_call" | custom-call | tf_op jit(solution)/shard_map/main_kernel/pallas_call | solution.py:833
  86.6 2.2 %finish_kernel.1 = (f32[8,16]{1,0:T(8,128)}, f32[256,128]{1,0:T(8,128)}, f32[256,128]{1,0:T(8,128)}, f32[1,128]{1,0:T(1,128)}, f32[1,128]{1,0:T(1,128)}, /*index...) custom-call(f32[8,128]{1,0:T(8,128)} %get-tuple-element.22.logits, ...), custom_call_target="tpu_custom_call" | custom-call | tf_op jit(solution)/shard_map/finish_kernel/pallas_call | solution.py:964
